TPU v7x, 32 devices: a whole 2x2x4 slice. The times are simulated.
32 devices in a mesh: slot: 8 (over y, x, core), seq: 4 (over z).
Axes of the slice: x: 2, y: 2, z: 4, core: 2. Of those that a mesh axis runs over, the one named last changes fastest.
Arguments:
- patches: bfloat16 [8, 1536, 768], P('slot', 'seq'), may hold values from -6 to 6
- segments: int32 [8, 1536], P('slot'), may hold values from 0 to 2, as said below
- code_bits: int32 [8, 1536, 18], P('slot', 'seq'), may hold values from 0 to 1
- norm_gain: bfloat16 [2, 2, 768], P(None, None, ('slot', 'seq')), may hold values from 0.5 to 1.5
- norm_shift: bfloat16 [2, 2, 768], P(None, None, ('slot', 'seq')), may hold values from -1.1953125 to 1.1953125
- project_weight: bfloat16 [2, 768, 2304], P(None, ('slot', 'seq')), may hold values from -0.3125 to 0.3125
- query_value_bias: bfloat16 [2, 2, 768], P(None, None, ('slot', 'seq')), may hold values from -1.1953125 to 1.1953125
- output_weight: bfloat16 [2, 768, 768], P(None, ('slot', 'seq')), may hold values from -0.625 to 0.625
- output_bias: bfloat16 [2, 768], P(None, ('slot', 'seq')), may hold values from -1.1953125 to 1.1953125
- expand_weight: bfloat16 [2, 768, 3072], P(None, ('slot', 'seq')), may hold values from -0.21875 to 0.21875
- expand_bias: bfloat16 [2, 3072], P(None, ('slot', 'seq')), may hold values from -1.1953125 to 1.1953125
- shrink_weight: bfloat16 [2, 3072, 768], P(None, ('slot', 'seq')), may hold values from -0.109375 to 0.109375
- shrink_bias: bfloat16 [2, 768], P(None, ('slot', 'seq')), may hold values from -1.1953125 to 1.1953125
- encode_weight: bfloat16 [768, 18], P(('slot', 'seq')), may hold values from -0.21875 to 0.21875
- decode_weight: bfloat16 [18, 768], P(None, ('slot', 'seq')), may hold values from -6 to 6
- decode_bias: bfloat16 [768], P(('slot', 'seq')), may hold values from -1.1953125 to 1.1953125
- cotangent: bfloat16 [8, 1536, 768], P('slot', 'seq'), may hold values from -6 to 6
Outputs:
- decoded: bfloat16 [8, 1536, 768], P('slot', 'seq')
- input_grad: float32 [8, 1536, 768], P('slot', 'seq')
- norm_gain_grad: float32 [2, 2, 768], P(None, None, ('slot', 'seq'))
- norm_shift_grad: float32 [2, 2, 768], P(None, None, ('slot', 'seq'))
- project_grad: float32 [2, 768, 2304], P(None, ('slot', 'seq'))
- query_value_grad: float32 [2, 2, 768], P(None, None, ('slot', 'seq'))
- output_weight_grad: float32 [2, 768, 768], P(None, ('slot', 'seq'))
- output_bias_grad: float32 [2, 768], P(None, ('slot', 'seq'))
- expand_weight_grad: float32 [2, 768, 3072], P(None, ('slot', 'seq'))
- expand_bias_grad: float32 [2, 3072], P(None, ('slot', 'seq'))
- shrink_weight_grad: float32 [2, 3072, 768], P(None, ('slot', 'seq'))
- shrink_bias_grad: float32 [2, 768], P(None, ('slot', 'seq'))
- encode_grad: float32 [768, 18], P(('slot', 'seq'))
- decode_grad: float32 [18, 768], P(None, ('slot', 'seq'))
- decode_bias_grad: float32 [768], P(('slot', 'seq'))
Inputs may be any that keep to these rules, and one draw needn't show every extreme that they name: `segments`: each slot holds three items numbered 0, 1, 2 in order of position; item 1 is 1024 patches long, begins within the first quarter of the slot and ends within the last quarter; items 0 and 2 are not empty.
All inputs are finite; a program needn't handle non-finite values.
Results may differ from a plain program's by a relative error of at most 0.02.
Values may be sent and summed in bfloat16 or wider, within the bound.
A program may use at most 256 MiB of HBM per device.

v0:
```python
import jax
import jax.numpy as jnp
from jax import lax
from jax.sharding import PartitionSpec as P

HD = 64
CODE = 18


epsilon = 1e-06
masked_score = -1000000000.0


def layer_norm(stream, gains, shifts):
    centre = stream - jnp.mean(stream, axis=-1, keepdims=True)
    spread = jnp.mean(centre * centre, axis=-1, keepdims=True)
    return centre * lax.rsqrt(spread + epsilon) * gains + shifts


def normalize(coded):
    return coded / jnp.sqrt(jnp.sum(coded * coded, axis=-1, keepdims=True) + epsilon)


def gelu_exact(hidden):
    return jax.nn.gelu(hidden, approximate=False)


def gather_weights(shards):
    return (
        lax.all_gather(shards[0], ("slot", "seq"), axis=2, tiled=True),
        lax.all_gather(shards[1], ("slot", "seq"), axis=2, tiled=True),
        lax.all_gather(shards[2], ("slot", "seq"), axis=1, tiled=True),
        lax.all_gather(shards[3], ("slot", "seq"), axis=2, tiled=True),
        lax.all_gather(shards[4], ("slot", "seq"), axis=1, tiled=True),
        lax.all_gather(shards[5], ("slot", "seq"), axis=1, tiled=True),
        lax.all_gather(shards[6], ("slot", "seq"), axis=1, tiled=True),
        lax.all_gather(shards[7], ("slot", "seq"), axis=1, tiled=True),
        lax.all_gather(shards[8], ("slot", "seq"), axis=1, tiled=True),
        lax.all_gather(shards[9], ("slot", "seq"), axis=1, tiled=True),
        lax.all_gather(shards[10], ("slot", "seq"), axis=0, tiled=True),
        lax.all_gather(shards[11], ("slot", "seq"), axis=1, tiled=True),
        lax.all_gather(shards[12], ("slot", "seq"), axis=0, tiled=True),
    )


def segment_mask(segments, offset, block_rows):
    return segments[:, None, offset : offset + block_rows, None] == segments[:, None, None, :]


def scaled_scores(queries, key_rows, same_item):
    scores = jnp.einsum("sqhd,skhd->shqk", queries, key_rows, preferred_element_type=jnp.float32)
    return jnp.where(same_item, scores * HD ** (-0.5), masked_score)


def forward_block(stream, layer, segments):
    (
        gains,
        shifts,
        project,
        query_value,
        output,
        output_shift,
        expand,
        expand_shift,
        shrink,
        shrink_shift,
    ) = layer
    slot_count, row_count, model_width = stream.shape
    seq_parts = lax.axis_size("seq")
    head_width = model_width // seq_parts
    normed = layer_norm(stream, gains[0].astype(jnp.float32), shifts[0].astype(jnp.float32)).astype(
        jnp.bfloat16
    )
    bias_row = jnp.concatenate(
        [query_value[0], jnp.zeros_like(query_value[0]), query_value[1]]
    ).astype(jnp.float32)
    projected = (jnp.dot(normed, project, preferred_element_type=jnp.float32) + bias_row).astype(
        jnp.bfloat16
    )
    split_heads = lax.all_to_all(
        projected.reshape(slot_count, row_count, 3, seq_parts, head_width),
        "seq",
        split_axis=3,
        concat_axis=1,
        tiled=True,
    )
    length = split_heads.shape[1]
    local_heads = head_width // HD
    queries = split_heads[:, :, 0, 0].reshape(slot_count, length, local_heads, HD)
    key_rows = split_heads[:, :, 1, 0].reshape(slot_count, length, local_heads, HD)
    values = split_heads[:, :, 2, 0].reshape(slot_count, length, local_heads, HD)
    block_rows = min(512, length)
    pieces = []
    log_parts = []
    for offset in range(0, length, block_rows):
        scores = scaled_scores(
            queries[:, offset : offset + block_rows],
            key_rows,
            segment_mask(segments, offset, block_rows),
        )
        row_top = jnp.max(scores, axis=-1, keepdims=True)
        raised = jnp.exp(scores - row_top)
        row_total = jnp.sum(raised, axis=-1, keepdims=True)
        probability = (raised / row_total).astype(jnp.bfloat16)
        pieces.append(
            jnp.einsum(
                "shqk,skhd->sqhd", probability, values, preferred_element_type=jnp.float32
            ).astype(jnp.bfloat16)
        )
        log_parts.append(row_top + jnp.log(row_total))
    log_sums = jnp.concatenate(log_parts, axis=2)
    attended = jnp.concatenate(pieces, axis=1).reshape(slot_count, length, 1, head_width)
    mixed_rows = lax.all_to_all(attended, "seq", split_axis=1, concat_axis=2, tiled=True).reshape(
        slot_count, row_count, model_width
    )
    middle = (
        stream
        + jnp.dot(mixed_rows, output, preferred_element_type=jnp.float32)
        + output_shift.astype(jnp.float32)
    )
    normed_mid = layer_norm(
        middle, gains[1].astype(jnp.float32), shifts[1].astype(jnp.float32)
    ).astype(jnp.bfloat16)
    hidden = jnp.dot(normed_mid, expand, preferred_element_type=jnp.float32) + expand_shift.astype(
        jnp.float32
    )
    active = gelu_exact(hidden).astype(jnp.bfloat16)
    result = (
        middle
        + jnp.dot(active, shrink, preferred_element_type=jnp.float32)
        + shrink_shift.astype(jnp.float32)
    )
    saved_values = (
        normed,
        queries,
        key_rows,
        values,
        log_sums,
        mixed_rows,
        middle,
        normed_mid,
        hidden,
        active,
    )
    return (result, saved_values)


def backward_block(grad_out, stream, saved_values, layer, segments):
    (
        gains,
        shifts,
        project,
        query_value,
        output,
        output_shift,
        expand,
        expand_shift,
        shrink,
        shrink_shift,
    ) = layer
    normed, queries, key_rows, values, log_sums, mixed_rows, middle, normed_mid, hidden, active = (
        saved_values
    )
    slot_count, row_count, model_width = stream.shape
    seq_parts = lax.axis_size("seq")
    head_width = model_width // seq_parts
    branch = grad_out.astype(jnp.bfloat16)
    shrink_shift_grad = jnp.sum(branch, axis=(0, 1), dtype=jnp.float32)
    shrink_grad = jnp.einsum("stf,sto->fo", active, branch, preferred_element_type=jnp.float32)
    active_grad = jnp.einsum("sto,fo->stf", branch, shrink, preferred_element_type=jnp.float32)
    unused, gelu_back = jax.vjp(gelu_exact, hidden)
    hidden_low = gelu_back(active_grad)[0].astype(jnp.bfloat16)
    expand_shift_grad = jnp.sum(hidden_low, axis=(0, 1), dtype=jnp.float32)
    expand_grad = jnp.einsum(
        "sti,stf->if", normed_mid, hidden_low, preferred_element_type=jnp.float32
    )
    normed_mid_grad = jnp.einsum(
        "stf,if->sti", hidden_low, expand, preferred_element_type=jnp.float32
    )
    unused, norm_back = jax.vjp(
        layer_norm, middle, gains[1].astype(jnp.float32), shifts[1].astype(jnp.float32)
    )
    middle_part, gain_mid_grad, shift_mid_grad = norm_back(normed_mid_grad)
    middle_grad = grad_out + middle_part
    branch_low = middle_grad.astype(jnp.bfloat16)
    output_shift_grad = jnp.sum(branch_low, axis=(0, 1), dtype=jnp.float32)
    output_grad = jnp.einsum(
        "sti,sto->io", mixed_rows, branch_low, preferred_element_type=jnp.float32
    )
    mixed_low = jnp.einsum(
        "sto,io->sti", branch_low, output, preferred_element_type=jnp.float32
    ).astype(jnp.bfloat16)
    head_grad = lax.all_to_all(
        mixed_low.reshape(slot_count, row_count, seq_parts, head_width),
        "seq",
        split_axis=2,
        concat_axis=1,
        tiled=True,
    )
    length = head_grad.shape[1]
    local_heads = head_width // HD
    head_grad = head_grad.reshape(slot_count, length, local_heads, HD)
    scale_factor = HD ** (-0.5)
    block_rows = min(512, length)
    key_grad = jnp.zeros((slot_count, length, local_heads, HD), jnp.float32)
    value_grad = jnp.zeros((slot_count, length, local_heads, HD), jnp.float32)
    query_parts = []
    for offset in range(0, length, block_rows):
        query_block = queries[:, offset : offset + block_rows]
        scores = scaled_scores(query_block, key_rows, segment_mask(segments, offset, block_rows))
        probability = jnp.exp(scores - log_sums[:, :, offset : offset + block_rows])
        out_grad = head_grad[:, offset : offset + block_rows]
        value_grad = value_grad + jnp.einsum(
            "shqk,sqhd->skhd",
            probability.astype(jnp.bfloat16),
            out_grad,
            preferred_element_type=jnp.float32,
        )
        prob_grad = jnp.einsum(
            "sqhd,skhd->shqk", out_grad, values, preferred_element_type=jnp.float32
        )
        centre = jnp.sum(probability * prob_grad, axis=-1, keepdims=True)
        score_low = (probability * (prob_grad - centre)).astype(jnp.bfloat16)
        query_parts.append(
            jnp.einsum("shqk,skhd->sqhd", score_low, key_rows, preferred_element_type=jnp.float32)
            * scale_factor
        )
        key_grad = (
            key_grad
            + jnp.einsum(
                "shqk,sqhd->skhd", score_low, query_block, preferred_element_type=jnp.float32
            )
            * scale_factor
        )
    query_grad = jnp.concatenate(query_parts, axis=1)
    joined = (
        jnp.stack([query_grad, key_grad, value_grad], axis=2)
        .astype(jnp.bfloat16)
        .reshape(slot_count, length, 3, 1, head_width)
    )
    project_low = lax.all_to_all(joined, "seq", split_axis=1, concat_axis=3, tiled=True).reshape(
        slot_count, row_count, 3 * model_width
    )
    project_shift = jnp.sum(project_low, axis=(0, 1), dtype=jnp.float32)
    query_value_grad = jnp.stack([project_shift[:model_width], project_shift[2 * model_width :]])
    project_grad = jnp.einsum(
        "sti,stj->ij", normed, project_low, preferred_element_type=jnp.float32
    )
    normed_grad = jnp.einsum(
        "stj,ij->sti", project_low, project, preferred_element_type=jnp.float32
    )
    unused, norm_back = jax.vjp(
        layer_norm, stream, gains[0].astype(jnp.float32), shifts[0].astype(jnp.float32)
    )
    stream_part, gain_in_grad, shift_in_grad = norm_back(normed_grad)
    input_part = middle_grad + stream_part
    grads = (
        jnp.stack([gain_in_grad, gain_mid_grad]),
        jnp.stack([shift_in_grad, shift_mid_grad]),
        project_grad,
        query_value_grad,
        output_grad,
        output_shift_grad,
        expand_grad,
        expand_shift_grad,
        shrink_grad,
        shrink_shift_grad,
    )
    return (input_part, grads)


def on_device(
    patches,
    segments,
    code_bits,
    norm_gain,
    norm_shift,
    project_weight,
    query_value_bias,
    output_weight,
    output_bias,
    expand_weight,
    expand_bias,
    shrink_weight,
    shrink_bias,
    encode_weight,
    decode_weight,
    decode_bias,
    cotangent,
):
    shards = (
        norm_gain,
        norm_shift,
        project_weight,
        query_value_bias,
        output_weight,
        output_bias,
        expand_weight,
        expand_bias,
        shrink_weight,
        shrink_bias,
        encode_weight,
        decode_weight,
        decode_bias,
    )
    gathered = gather_weights(shards)
    stream_in = patches.astype(jnp.float32)
    encoded, unused = forward_block(
        stream_in, tuple((array[0] for array in gathered[:10])), segments
    )
    encoded_low = encoded.astype(jnp.bfloat16)
    coded = jnp.einsum("sti,ic->stc", encoded_low, gathered[10], preferred_element_type=jnp.float32)
    signs = ((2 * code_bits - 1).astype(jnp.float32) * CODE ** (-0.5)).astype(jnp.bfloat16)
    start = jnp.einsum(
        "stc,ci->sti", signs, gathered[11], preferred_element_type=jnp.float32
    ) + gathered[12].astype(jnp.float32)
    decoded, decoder_saved = forward_block(
        start, tuple((array[1] for array in gathered[:10])), segments
    )
    weights_back = gather_weights(shards)
    encoder = tuple((array[0] for array in weights_back[:10]))
    decoder = tuple((array[1] for array in weights_back[:10]))
    start_grad, decoder_grads = backward_block(
        cotangent.astype(jnp.float32), start, decoder_saved, decoder, segments
    )
    start_low = start_grad.astype(jnp.bfloat16)
    decode_bias_grad = jnp.sum(start_low, axis=(0, 1), dtype=jnp.float32)
    decode_grad = jnp.einsum("stc,sti->ci", signs, start_low, preferred_element_type=jnp.float32)
    unit_grad = jnp.einsum(
        "sti,ci->stc", start_low, weights_back[11], preferred_element_type=jnp.float32
    )
    unit_rows, unit_back = jax.vjp(normalize, coded)
    coded_low = unit_back(unit_grad)[0].astype(jnp.bfloat16)
    encode_grad = jnp.einsum(
        "sti,stc->ic", encoded_low, coded_low, preferred_element_type=jnp.float32
    )
    encoded_grad = jnp.einsum(
        "stc,ic->sti", coded_low, weights_back[10], preferred_element_type=jnp.float32
    )
    unused, encoder_saved = forward_block(stream_in, encoder, segments)
    input_grad, encoder_grads = backward_block(
        encoded_grad, stream_in, encoder_saved, encoder, segments
    )
    pairs = tuple(
        (jnp.stack([first, second]) for first, second in zip(encoder_grads, decoder_grads))
    )
    totals = (
        lax.psum_scatter(pairs[0], ("slot", "seq"), scatter_dimension=2, tiled=True),
        lax.psum_scatter(pairs[1], ("slot", "seq"), scatter_dimension=2, tiled=True),
        lax.psum_scatter(pairs[2], ("slot", "seq"), scatter_dimension=1, tiled=True),
        lax.psum_scatter(pairs[3], ("slot", "seq"), scatter_dimension=2, tiled=True),
        lax.psum_scatter(pairs[4], ("slot", "seq"), scatter_dimension=1, tiled=True),
        lax.psum_scatter(pairs[5], ("slot", "seq"), scatter_dimension=1, tiled=True),
        lax.psum_scatter(pairs[6], ("slot", "seq"), scatter_dimension=1, tiled=True),
        lax.psum_scatter(pairs[7], ("slot", "seq"), scatter_dimension=1, tiled=True),
        lax.psum_scatter(pairs[8], ("slot", "seq"), scatter_dimension=1, tiled=True),
        lax.psum_scatter(pairs[9], ("slot", "seq"), scatter_dimension=1, tiled=True),
        lax.psum_scatter(encode_grad, ("slot", "seq"), scatter_dimension=0, tiled=True),
        lax.psum_scatter(decode_grad, ("slot", "seq"), scatter_dimension=1, tiled=True),
        lax.psum_scatter(decode_bias_grad, ("slot", "seq"), scatter_dimension=0, tiled=True),
    )
    return (decoded.astype(jnp.bfloat16), input_grad) + tuple(totals)


def solution(mesh):
    in_specs = (
        P("slot", "seq", None),
        P("slot", None),
        P("slot", "seq", None),
        P(None, None, ("slot", "seq")),
        P(None, None, ("slot", "seq")),
        P(None, ("slot", "seq"), None),
        P(None, None, ("slot", "seq")),
        P(None, ("slot", "seq"), None),
        P(None, ("slot", "seq")),
        P(None, ("slot", "seq"), None),
        P(None, ("slot", "seq")),
        P(None, ("slot", "seq"), None),
        P(None, ("slot", "seq")),
        P(("slot", "seq"), None),
        P(None, ("slot", "seq")),
        P(("slot", "seq")),
        P("slot", "seq", None),
    )
    out_specs = (
        P("slot", "seq", None),
        P("slot", "seq", None),
        P(None, None, ("slot", "seq")),
        P(None, None, ("slot", "seq")),
        P(None, ("slot", "seq"), None),
        P(None, None, ("slot", "seq")),
        P(None, ("slot", "seq"), None),
        P(None, ("slot", "seq")),
        P(None, ("slot", "seq"), None),
        P(None, ("slot", "seq")),
        P(None, ("slot", "seq"), None),
        P(None, ("slot", "seq")),
        P(("slot", "seq"), None),
        P(None, ("slot", "seq")),
        P(("slot", "seq")),
    )
    return jax.shard_map(
        on_device, mesh=mesh, in_specs=in_specs, out_specs=out_specs, check_vma=False
    )
```

profile of v0, /device:TPU:0, one launch (start us, length us, event | category | flops | bytes accessed | tf_op | source)
XLA Modules:
  0.0 2216.6 jit_solution(10602095630113695622)
XLA Ops:
  10.8 72.9 %all_gather.50 = bf16[18,768]{0,1:T(8,128)(2,1)S(1)} all-gather(bf16[18,24]{0,1:T(8,128)(2,1)S(1)} %copy.101), channel_id=1, replica_groups=mesh['slot'=8,'seq'=4] {'slot','seq'}, dimensions={1}, use_global_device_ids=true | all-gather | bytes 28512 | tf_op jit(solution)/shard_map/all_gather | solution.py:41
  85.5 37.0 %all-reduce = bf16[768]{0:T(1024)(128)(2,1)S(1)} all-reduce(bf16[768]{0:T(1024)(128)(2,1)S(1)} %dynamic-update-slice), channel_id=1, replica_groups=mesh['slot'=8,'seq'=4] {'slot','seq'}, use_global_device_ids=true, to_apply=%add | all-reduce | flops 768 | bytes 3072
  124.7 71.7 %all_gather.55 = bf16[2,2,768]{1,0,2:T(2,128)(2,1)S(1)} all-gather(bf16[2,2,24]{1,0,2:T(2,128)(2,1)S(1)} %copy.104), channel_id=1, replica_groups=mesh['slot'=8,'seq'=4] {'slot','seq'}, dimensions={2}, use_global_device_ids=true | all-gather | bytes 6336 | tf_op jit(solution)/shard_map/all_gather | solution.py:33
  196.4 9.9 slice_reduce_fusion.1
  206.4 69.7 %all_gather.52 = bf16[2,2,768]{1,0,2:T(2,128)(2,1)S(1)} all-gather(bf16[2,2,24]{1,0,2:T(2,128)(2,1)S(1)} %copy.102), channel_id=1, replica_groups=mesh['slot'=8,'seq'=4] {'slot','seq'}, dimensions={2}, use_global_device_ids=true | all-gather | bytes 6336 | tf_op jit(solution)/shard_map/all_gather | solution.py:30
  276.1 8.9 fusion.143
  285.1 71.5 %all_gather.53 = bf16[2,2,768]{1,0,2:T(2,128)(2,1)S(1)} all-gather(bf16[2,2,24]{1,0,2:T(2,128)(2,1)S(1)} %copy.103), channel_id=1, replica_groups=mesh['slot'=8,'seq'=4] {'slot','seq'}, dimensions={2}, use_global_device_ids=true | all-gather | bytes 6336 | tf_op jit(solution)/shard_map/all_gather | solution.py:31
  356.6 8.9 fusion.142
  365.5 63.0 %all-gather = bf16[32,24,2]{1,2,0:T(2,128)(2,1)S(1)} all-gather(bf16[1,24,2]{1,2,0:T(2,128)(2,1)S(1)} %bitcast.596), channel_id=1, replica_groups=mesh['slot'=8,'seq'=4] {'slot','seq'}, dimensions={0}, use_global_device_ids=true | all-gather | bytes 3168 | tf_op jit(solution)/shard_map/all_gather | solution.py:35
  429.2 65.2 %all-gather.1 = bf16[32,96,2]{1,2,0:T(2,128)(2,1)S(1)} all-gather(bf16[1,96,2]{1,2,0:T(2,128)(2,1)S(1)} %bitcast.597), channel_id=1, replica_groups=mesh['slot'=8,'seq'=4] {'slot','seq'}, dimensions={0}, use_global_device_ids=true | all-gather | bytes 12672 | tf_op jit(solution)/shard_map/all_gather | solution.py:37
  495.2 63.0 %all-gather.2 = bf16[32,24,2]{1,2,0:T(2,128)(2,1)S(1)} all-gather(bf16[1,24,2]{1,2,0:T(2,128)(2,1)S(1)} %bitcast.598), channel_id=1, replica_groups=mesh['slot'=8,'seq'=4] {'slot','seq'}, dimensions={0}, use_global_device_ids=true | all-gather | bytes 3168 | tf_op jit(solution)/shard_map/all_gather | solution.py:39
  572.8 100.5 %all_gather.62 = bf16[768,18]{1,0:T(8,128)(2,1)} all-gather(bf16[24,18]{1,0:T(8,128)(2,1)} %param.30), channel_id=1, replica_groups=mesh['slot'=8,'seq'=4] {'slot','seq'}, dimensions={0}, use_global_device_ids=true | all-gather | bytes 28512 | tf_op jit(solution)/shard_map/all_gather | solution.py:40
  709.5 8.5 fusion.1
  733.5 10.8 reduce.121
  785.6 8.9 reduce.122
  822.5 15.5 multiply_convert_fusion.7
  838.0 8.5 convert_reduce_fusion
  861.3 8.5 all-to-all-done.2
  874.5 8.5 multiply_reduce_fusion.5
  961.9 15.4 multiply_convert_fusion.6
  983.4 41.3 %all-to-all-done.3 = bf16[1,1536,3,1,192]{4,2,3,0,1:T(4,128)(2,1)} async-done(((bf16[1,1536,3,1,192]{4,2,3,0,1:T(4,128)(2,1)}), bf16[1,1536,3,1,192]{4,2,3,0,1:T(4,128)(2,1)}, u32[]{:S(2)}, u32[]{:S(2)}) %all-to-all-start.3) | async-done | bytes 1769504 | tf_op jit(solution)/shard_map/all_to_all | solution.py:241
  1058.7 15.2 all-to-all-done.6
  1077.5 8.5 multiply_reduce_fusion.2
  1143.8 8.3 pad_maximum_fusion.5
  1167.8 61.7 %all-to-all-done.7 = bf16[1,1536,3,1,192]{4,2,3,0,1:T(4,128)(2,1)} async-done(((bf16[1,1536,3,1,192]{4,2,3,0,1:T(4,128)(2,1)}), bf16[1,1536,3,1,192]{4,2,3,0,1:T(4,128)(2,1)}, u32[]{:S(2)}, u32[]{:S(2)}) %all-to-all-start.7) | async-done | bytes 1769504 | tf_op jit(solution)/shard_map/all_to_all | solution.py:241
  1270.3 10.9 pad_maximum_fusion.2
  1323.1 80.4 %all-reduce.12.cloned.1.call-done = (f32[2,2,768]{2,1,0:T(2,128)}, f32[2,2,768]{2,1,0:T(2,128)}, f32[2,2,768]{2,1,0:T(2,128)}, f32[2,768]{1,0:T(2,128)}, f32[2,7...) async-done(((f32[2,2,768]{2,1,0:T(2,128)}, f32[2,2,768]{2,1,0:T(2,128)}, f32[2,2,768]{2,1,0:T(2,128)}, f32[2,768]{1,0:T(2,128)}, f32[2,768]{1,0:T(2,128)}, ...) | async-done | bytes 107536
  1412.8 91.4 %reduce-scatter.27.cloned.1.call-done = f32[24,18]{1,0:T(8,128)} async-done(((f32[768,18]{1,0:T(8,128)}), f32[24,18]{1,0:T(8,128)}) %reduce-scatter.27.cloned.1.call-update) | async-done | bytes 1744
  1504.3 112.2 %reduce-scatter.19.cloned.1.call-done = f32[2,24,768]{2,1,0:T(8,128)} async-done(((f32[2,768,768]{2,1,0:T(8,128)}), f32[2,24,768]{2,1,0:T(8,128)}) %reduce-scatter.19.cloned.1.call-update) | async-done | bytes 147472 | tf_op jit(solution)/shard_map/reduce_scatter | solution.py:352
  1616.4 169.7 %reduce-scatter.17.cloned.1.call-done = f32[2,24,2304]{2,1,0:T(8,128)} async-done(((f32[2,768,2304]{2,1,0:T(8,128)}), f32[2,24,2304]{2,1,0:T(8,128)}) %reduce-scatter.17.cloned.1.call-update) | async-done | bytes 442384 | tf_op jit(solution)/shard_map/reduce_scatter | solution.py:350
  1786.1 211.7 %reduce-scatter.23.cloned.1.call-done = f32[2,96,768]{2,1,0:T(8,128)} async-done(((f32[2,3072,768]{2,1,0:T(8,128)}), f32[2,96,768]{2,1,0:T(8,128)}) %reduce-scatter.23.cloned.1.call-update) | async-done | bytes 589840 | tf_op jit(solution)/shard_map/reduce_scatter | solution.py:356
  1997.8 212.1 %reduce-scatter.21.cloned.1.call-done = f32[2,24,3072]{2,1,0:T(8,128)} async-done(((f32[2,768,3072]{2,1,0:T(8,128)}), f32[2,24,3072]{2,1,0:T(8,128)}) %reduce-scatter.21.cloned.1.call-update) | async-done | bytes 589840 | tf_op jit(solution)/shard_map/reduce_scatter | solution.py:354
  (605 shorter events, 450.0 us)
Async XLA Ops:
  7.2 553.0 %all-gather.8.cloned.1.call-start = ((), (), s32[]{:S(2)}) async-start(), calls=%async_computation.14 | async-start | bytes 7299072 | tf_op jit(solution)/shard_map/all_gather | solution.py:32
  7.9 812.2 %all-gather.10.cloned.1.call-start = ((), (), s32[]{:S(2)}) async-start(), calls=%async_computation.15 | async-start | bytes 2433024 | tf_op jit(solution)/shard_map/all_gather | solution.py:34
  8.7 356.8 %copy-start.142 = (bf16[2,24]{1,0:T(2,128)(2,1)S(1)}, bf16[2,24]{1,0:T(2,128)(2,1)}, u32[]{:S(2)}) copy-start(bf16[2,24]{1,0:T(2,128)(2,1)} %param.25) | copy-start | bytes 292
  8.7 420.5 %copy-start.143 = (bf16[2,96]{1,0:T(2,128)(2,1)S(1)}, bf16[2,96]{1,0:T(2,128)(2,1)}, u32[]{:S(2)}) copy-start(bf16[2,96]{1,0:T(2,128)(2,1)} %param.27) | copy-start | bytes 1156
  8.7 813.7 %all-gather.12.cloned.1.call-start = ((), (), s32[]{:S(2)}) async-start(), calls=%async_computation.16 | async-start | bytes 9732096 | tf_op jit(solution)/shard_map/all_gather | solution.py:36
  9.4 485.6 %copy-start.34 = (bf16[1,384,768]{2,1,0:T(8,128)(2,1)S(1)}, bf16[1,384,768]{2,1,0:T(8,128)(2,1)}, u32[]{:S(2)}) copy-start(bf16[1,384,768]{2,1,0:T(8,128)(2,1)} %param.17) | copy-start | bytes 1769476
  9.5 828.6 %all-gather.14.cloned.1.call-start = ((), (), s32[]{:S(2)}) async-start(), calls=%async_computation.17 | async-start | bytes 9732096 | tf_op jit(solution)/shard_map/all_gather | solution.py:38
  83.8 474.5 %copy-start.70 = (bf16[18,768]{0,1:T(8,128)(2,1)}, bf16[18,768]{0,1:T(8,128)(2,1)S(1)}, u32[]{:S(2)}) copy-start(bf16[18,768]{0,1:T(8,128)(2,1)S(1)} %all_gather.50) | copy-start | bytes 82948
  83.8 411.5 %copy-start.144 = (bf16[2,24]{1,0:T(2,128)(2,1)S(1)}, bf16[2,24]{1,0:T(2,128)(2,1)}, u32[]{:S(2)}) copy-start(bf16[2,24]{1,0:T(2,128)(2,1)} %param.29) | copy-start | bytes 292
  84.6 474.3 %copy-start.82 = (bf16[1,384,18]{1,0,2:T(2,128)(2,1)}, bf16[1,384,18]{1,0,2:T(2,128)(2,1)S(1)}, u32[]{:S(2)}) copy-start(bf16[1,384,18]{1,0,2:T(2,128)(2,1)S(1)} %multiply_convert_fusion.8) | copy-start | bytes 41476
  85.5 473.5 %copy-start.124 = (s32[1,1536]{1,0:T(1,128)S(1)}, s32[1,1536]{1,0:T(1,128)}, u32[]{:S(2)}) copy-start(s32[1,1536]{1,0:T(1,128)} %param.18) | copy-start | bytes 18436
  122.9 697.2 %copy-start.10 = (f32[384,768]{1,0:T(8,128)}, f32[384,768]{1,0:T(8,128)S(1)}, u32[]{:S(2)}) copy-start(f32[384,768]{1,0:T(8,128)S(1)} %get-tuple-element.88) | copy-start | bytes 3538948
  122.9 437.3 %copy-start.99 = (f32[384]{0:T(512)}, f32[384]{0:T(512)S(1)}, u32[]{:S(2)}) copy-start(f32[384]{0:T(512)S(1)} %broadcast_multiply_fusion.3) | copy-start | bytes 4612
  123.9 436.3 %copy-start.110 = (f32[384]{0:T(512)}, f32[384]{0:T(512)S(1)}, u32[]{:S(2)}) copy-start(f32[384]{0:T(512)S(1)} %fusion.172) | copy-start | bytes 4612
  285.0 394.3 %copy-start.104 = (f32[768]{0:T(1024)}, f32[768]{0:T(1024)S(1)}, u32[]{:S(2)}) copy-start(f32[768]{0:T(1024)S(1)} %get-tuple-element.26) | copy-start | bytes 9220
  285.0 564.3 %copy-start.76 = (f32[768]{0:T(1024)}, f32[768]{0:T(1024)S(1)}, u32[]{:S(2)}) copy-start(f32[768]{0:T(1024)S(1)} %get-tuple-element.27) | copy-start | bytes 9220
  365.5 457.0 %copy-start.80 = (f32[768]{0:T(1024)}, f32[768]{0:T(1024)S(1)}, u32[]{:S(2)}) copy-start(f32[768]{0:T(1024)S(1)} %get-tuple-element.31) | copy-start | bytes 9220
  569.2 121.7 %all-to-all-start = ((bf16[1,384,3,4,192]{1,4,2,0,3:T(8,128)(2,1)}), bf16[1,384,3,4,192]{1,4,2,0,3:T(8,128)(2,1)S(1)}, u32[]{:S(2)}, u32[]{:S(2)}) async-start(bf16[1,384,3,4,192]{1,4,2,0,3:T(8,128)(2,1)} %copy.106), calls=%async_computation | async-start | bytes 3538944 | tf_op jit(solution)/shard_map/all_to_all | solution.py:80
  692.1 55.3 %all-to-all-start.4 = ((bf16[1,384,3,4,192]{1,4,2,0,3:T(8,128)(2,1)}), bf16[1,384,3,4,192]{1,4,2,0,3:T(8,128)(2,1)S(1)}, u32[]{:S(2)}, u32[]{:S(2)}) async-start(bf16[1,384,3,4,192]{1,4,2,0,3:T(8,128)(2,1)} %copy.123), calls=%async_computation.4 | async-start | bytes 3538944 | tf_op jit(solution)/shard_map/all_to_all | solution.py:80
  747.4 48.8 %all-to-all-start.1 = ((bf16[4,2,36864]{2,1,0:T(2,128)(2,1)}), bf16[4,2,36864]{2,1,0:T(2,128)(2,1)}, u32[]{:S(2)}, u32[]{:S(2)}) async-start(bf16[4,2,36864]{2,1,0:T(2,128)(2,1)} %reshape.1645), calls=%async_computation.1 | async-start | bytes 1179648 | tf_op jit(solution)/shard_map/all_to_all | solution.py:113
  796.2 16.2 all-to-all-start.5
  854.3 15.5 all-to-all-start.2
  956.6 68.1 %all-to-all-start.3 = ((bf16[1,1536,3,1,192]{4,2,3,0,1:T(4,128)(2,1)}), bf16[1,1536,3,1,192]{4,2,3,0,1:T(4,128)(2,1)}, u32[]{:S(2)}, u32[]{:S(2)}) async-start(bf16[1,1536,3,1,192]{4,2,3,0,1:T(4,128)(2,1)} %pad_maximum_fusion.4), calls=%async_computation.3 | async-start | bytes 6291456 | tf_op jit(solution)/shard_map/all_to_all | solution.py:241
  1054.9 19.0 all-to-all-start.6
  1152.1 77.4 %all-to-all-start.7 = ((bf16[1,1536,3,1,192]{4,2,3,0,1:T(4,128)(2,1)}), bf16[1,1536,3,1,192]{4,2,3,0,1:T(4,128)(2,1)}, u32[]{:S(2)}, u32[]{:S(2)}) async-start(bf16[1,1536,3,1,192]{4,2,3,0,1:T(4,128)(2,1)} %pad_maximum_fusion.5), calls=%async_computation.7 | async-start | bytes 6291456 | tf_op jit(solution)/shard_map/all_to_all | solution.py:241
  1156.9 161.1 %reduce-scatter.25.cloned.1.call-start = ((), (), s32[]{:S(2)}) async-start(), calls=%async_computation.22 | async-start | bytes 1622016
  1161.0 242.5 %all-reduce.12.cloned.1.call-start = ((), (), s32[]{:S(2)}) async-start(), calls=%async_computation.24 | async-start | bytes 253952
  1249.1 255.1 %reduce-scatter.27.cloned.1.call-start = ((), (), s32[]{:S(2)}) async-start(), calls=%async_computation.23 | async-start | bytes 405504
  1252.6 363.8 %reduce-scatter.19.cloned.1.call-start = ((), (), s32[]{:S(2)}) async-start(), calls=%async_computation.19 | async-start | bytes 4866048 | tf_op jit(solution)/shard_map/reduce_scatter | solution.py:352
  1257.6 528.5 %reduce-scatter.17.cloned.1.call-start = ((), (), s32[]{:S(2)}) async-start(), calls=%async_computation.18 | async-start | bytes 14598144 | tf_op jit(solution)/shard_map/reduce_scatter | solution.py:350
  1281.2 716.6 %reduce-scatter.23.cloned.1.call-start = ((), (), s32[]{:S(2)}) async-start(), calls=%async_computation.21 | async-start | bytes 19464192 | tf_op jit(solution)/shard_map/reduce_scatter | solution.py:356
  1296.2 913.7 %reduce-scatter.21.cloned.1.call-start = ((), (), s32[]{:S(2)}) async-start(), calls=%async_computation.20 | async-start | bytes 19464192 | tf_op jit(solution)/shard_map/reduce_scatter | solution.py:354
  (156 other events, 2783.0 us)
Sparse Core Ops, SparseCore 0:
  11.1 75.9 all-gather.7
  90.1 56.3 all-gather.9
  149.6 83.2 all-gather.11
  235.8 83.1 all-gather.13
  1162.7 109.6 reduce-scatter.24
  1279.3 124.2 all-reduce.11
  1409.8 94.3 reduce-scatter.26
  1510.3 106.0 reduce-scatter.18
  1624.1 162.0 reduce-scatter.16
  1794.1 203.6 reduce-scatter.22
  2005.9 203.9 reduce-scatter.20
where the time goes:
time: 2230 us; the launch traced here: 2220 us
  waiting for transfers between devices  1010 us (45%)
  blocking collectives  614 us (28%)
  matrix products  252 us (11%)
  other arithmetic  161 us (7%)
  local copies, waits for them, and re-layouts  125 us (6%)
  starting transfers between devices  36.9 us (2%)
    reduce_scatter x1, waiting for transfers between devices, on_device(): lax.psum_scatter(pairs[6], ('slot', 'seq'), scatter_dimension=1, tiled=True)  212 us
    reduce_scatter x1, waiting for transfers between devices, on_device(): lax.psum_scatter(pairs[8], ('slot', 'seq'), scatter_dimension=1, tiled=True)  212 us
    unnamed x14, waiting for transfers between devices  175 us
    reduce_scatter x1, waiting for transfers between devices, on_device(): lax.psum_scatter(pairs[2], ('slot', 'seq'), scatter_dimension=1, tiled=True)  170 us
    reduce_scatter x1, waiting for transfers between devices, on_device(): lax.psum_scatter(pairs[4], ('slot', 'seq'), scatter_dimension=1, tiled=True)  112 us
    all_to_all x2, waiting for transfers between devices, backward_block(): lax.all_to_all(joined, 'seq', split_axis=1, concat_axis=3, tiled=True)  103 us
    all_gather x1, blocking collectives, gather_weights(): lax.all_gather(shards[10], ('slot', 'seq'), axis=0, tiled=True)  100 us
    all_gather x1, blocking collectives, gather_weights(): lax.all_gather(shards[11], ('slot', 'seq'), axis=1, tiled=True)  72.9 us
  transfers between devices with their start and end apart: 19, of which 11 were waited for; matrix products, arithmetic and copies ran while one was open for 14% of the time, Pallas kernels for 0%

commit v1 on v0

--- a/solution.py
+++ b/solution.py
@@ -1,17 +1,1371 @@
+import functools
+
 import jax
 import jax.numpy as jnp
 from jax import lax
+from jax.experimental import pallas as pl
+from jax.experimental.pallas import tpu as pltpu
 from jax.sharding import PartitionSpec as P
 
 HD = 64
 CODE = 18
-
-
 epsilon = 1e-06
 masked_score = -1000000000.0
-
-
-def layer_norm(stream, gains, shifts):
+MESH = pl.DeviceIdType.MESH
+F32 = jnp.float32
+BF16 = jnp.bfloat16
+AXES = ("slot", "seq")
+BIG = 60 * 1024 * 1024
+
+NN = (((1,), (0,)), ((), ()))
+NT = (((1,), (1,)), ((), ()))
+TN = (((0,), (0,)), ((), ()))
+
+
+def mm(a, b, dims=NN):
+    return lax.dot_general(a, b, dims, preferred_element_type=F32)
+
+
+def params(**more):
+    return pltpu.CompilerParams(vmem_limit_bytes=BIG, **more)
+
+
+def whole(shape):
+    return pl.BlockSpec(shape, lambda *i: (0,) * len(shape))
+
+
+def shaped(shape, dtype=BF16):
+    return jax.ShapeDtypeStruct(shape, dtype)
+
+
+def norm_parts(stream):
+    centre = stream - jnp.mean(stream, axis=-1, keepdims=True)
+    spread = jnp.mean(centre * centre, axis=-1, keepdims=True)
+    scale = lax.rsqrt(spread + epsilon)
+    return centre * scale, scale
+
+
+def norm_back(grad, gain, hat, scale):
+    lifted = grad * gain
+    mean = jnp.mean(lifted, axis=-1, keepdims=True)
+    mixed = jnp.mean(lifted * hat, axis=-1, keepdims=True)
+    return scale * (lifted - mean - hat * mixed)
+
+
+def columns(value):
+    return jnp.sum(value, axis=0, keepdims=True)
+
+
+def lanes_of(head):
+    lane = lax.broadcasted_iota(jnp.int32, (1, 2 * HD), 1)
+    return lane < HD if head == 0 else lane >= HD
+
+
+def only(value, head):
+    return jnp.where(lanes_of(head), value, jnp.zeros_like(value))
+
+
+def gelu_parts(hidden):
+    normal = 0.5 + 0.5 * lax.erf(hidden * 0.7071067811865476)
+    density = jnp.exp(-0.5 * hidden * hidden) * 0.3989422804014327
+    return hidden * normal, normal + hidden * density
+
+
+def flip(index, bit):
+    size = 1 << bit
+    return index + size - 2 * size * ((index // size) % 2)
+
+
+def relative(a, b):
+    return 2 * ((a // 2 + b // 2) % 2) + (a + b) % 2
+
+
+PARTS = 4
+DMA = pltpu.SemaphoreType.DMA
+
+
+def remote(src, dst, send, recv, peer):
+    return pltpu.make_async_remote_copy(
+        src_ref=src, dst_ref=dst, send_sem=send, recv_sem=recv, device_id=peer, device_id_type=MESH
+    )
+
+
+class Here:
+    def __init__(self):
+        self.slot, self.z = lax.axis_index("slot"), lax.axis_index("seq")
+        self.across = (flip(self.slot, 1), self.z)
+        self.beside = (flip(self.slot, 2), self.z)
+        self.sibling = (flip(self.slot, 0), self.z)
+        self.core, self.square = lax.rem(self.slot, 2), self.slot // 2
+
+    def along(self, k):
+        return (self.slot, relative(self.z, k))
+
+    def greet(self):
+        barrier = pltpu.get_barrier_semaphore()
+        peers = [self.across, self.beside, self.sibling] + [self.along(k) for k in range(1, PARTS)]
+        for peer in peers:
+            pl.semaphore_signal(barrier, inc=1, device_id=peer, device_id_type=MESH)
+        pl.semaphore_wait(barrier, len(peers))
+
+
+class Line:
+    @staticmethod
+    def scratch(count):
+        return [DMA((count, PARTS))] * 3
+
+    def __init__(self, here, arrays, sems):
+        self.here, self.arrays = here, arrays
+        self.recv, self.up, self.down = sems
+
+    def copy(self, m, block, upward):
+        z = self.here.z
+        to = jnp.minimum(z + 1, PARTS - 1) if upward else jnp.maximum(z - 1, 0)
+        array = self.arrays[m]
+        send = (self.up if upward else self.down).at[m, block]
+        return remote(
+            array.at[relative(block, z)], array.at[relative(block, to)], send, self.recv.at[m, block], (self.here.slot, to)
+        )
+
+    def onward(self, m, block, upward):
+        z = self.here.z
+
+        @pl.when((z < PARTS - 1) if upward else (z > 0))
+        def _():
+            self.copy(m, block, upward).start()
+
+    def start(self, m):
+        self.onward(m, self.here.z, True)
+        self.onward(m, self.here.z, False)
+
+    def hop(self, m, k):
+        z = self.here.z
+
+        @pl.when(z >= k)
+        def _():
+            self.copy(m, z - k, True).wait_recv()
+            self.onward(m, z - k, True)
+
+        @pl.when(z + k <= PARTS - 1)
+        def _():
+            self.copy(m, z + k, False).wait_recv()
+            self.onward(m, z + k, False)
+
+    def finish(self, m):
+        z = self.here.z
+        for block in range(PARTS):
+
+            @pl.when((z < PARTS - 1) & (z >= block))
+            def _():
+                self.copy(m, block, True).wait_send()
+
+            @pl.when((z > 0) & (z <= block))
+            def _():
+                self.copy(m, block, False).wait_send()
+
+
+class Gather:
+    @staticmethod
+    def scratch(count):
+        return [DMA((count, PARTS))] * 5 + [DMA((count,))] * 8
+
+    def __init__(self, here, sources, outs, sems):
+        self.here, self.sources, self.outs = here, sources, outs
+        self.rz, self.up, self.down, self.rx, self.ry = sems[:5]
+        self.local, self.sx, self.sy, self.rd, self.dx, self.dy, self.rc, self.sc = sems[5:]
+
+    def place(self, m, block):
+        return self.outs[m].at[self.here.slot, block]
+
+    def copy(self, m, block, upward, src):
+        z = self.here.z
+        to = jnp.minimum(z + 1, PARTS - 1) if upward else jnp.maximum(z - 1, 0)
+        send = (self.up if upward else self.down).at[m, block]
+        return remote(src, self.place(m, block), send, self.rz.at[m, block], (self.here.slot, to))
+
+    def onward(self, m, block, upward, src):
+        z = self.here.z
+
+        @pl.when((z < PARTS - 1) if upward else (z > 0))
+        def _():
+            self.copy(m, block, upward, src).start()
+
+    def sideways(self, m, block, src):
+        dst = self.place(m, block)
+        remote(src, dst, self.sx.at[m], self.rx.at[m, block], self.here.across).start()
+        remote(src, dst, self.sy.at[m], self.ry.at[m, block], self.here.beside).start()
+
+    def keep(self, m):
+        return pltpu.make_async_copy(self.sources[m], self.place(m, self.here.z), self.local.at[m])
+
+    def start(self, m):
+        src, z = self.sources[m], self.here.z
+        self.onward(m, z, True, src)
+        self.onward(m, z, False, src)
+        self.sideways(m, z, src)
+        self.keep(m).start()
+
+    def arrived(self, m, block, upward):
+        src = self.place(m, block)
+        self.copy(m, block, upward, src).wait_recv()
+        self.onward(m, block, upward, src)
+        self.sideways(m, block, src)
+
+    def hop(self, m, k):
+        z = self.here.z
+
+        @pl.when(z >= k)
+        def _():
+            self.arrived(m, z - k, True)
+
+        @pl.when(z + k <= PARTS - 1)
+        def _():
+            self.arrived(m, z + k, False)
+
+    def turned(self, m, block):
+        across, beside = self.here.across, self.here.beside
+        here = self.outs[m].at[across[0], block]
+        remote(here, here, self.sx.at[m], self.rx.at[m, block], across).wait_recv()
+
+        @pl.when(lax.rem(block, 2) == 0)
+        def _():
+            remote(here, here, self.dy.at[m], self.rd.at[m], beside).start()
+
+        there = self.outs[m].at[beside[0], block]
+        remote(there, there, self.sy.at[m], self.ry.at[m, block], beside).wait_recv()
+
+        @pl.when(lax.rem(block, 2) == 1)
+        def _():
+            remote(there, there, self.dx.at[m], self.rd.at[m], across).start()
+
+    def turn(self, m, k):
+        z = self.here.z
+        if k == 0:
+            self.turned(m, z)
+            return
+
+        @pl.when(z >= k)
+        def _():
+            self.turned(m, z - k)
+
+        @pl.when(z + k <= PARTS - 1)
+        def _():
+            self.turned(m, z + k)
+
+    def share(self, m, slot):
+        group = self.outs[m].at[slot]
+        remote(group, group, self.sc.at[m], self.rc.at[m], self.here.sibling).start()
+
+    def siblings(self, m):
+        self.keep(m).wait()
+        for slot in (self.here.slot, self.here.across[0], self.here.beside[0]):
+            self.share(m, slot)
+
+    def corner(self, m):
+        slot = flip(self.here.across[0], 2)
+        group = self.outs[m].at[slot]
+        remote(group, group, self.dx.at[m], self.rd.at[m], self.here.across).wait_recv()
+        self.share(m, slot)
+
+    def finish(self, m):
+        here, z, src = self.here, self.here.z, self.sources[m]
+        for block in range(PARTS):
+
+            @pl.when((z < PARTS - 1) & (z >= block))
+            def _():
+                self.copy(m, block, True, src).wait_send()
+
+            @pl.when((z > 0) & (z <= block))
+            def _():
+                self.copy(m, block, False, src).wait_send()
+
+        group = self.outs[m].at[here.slot]
+        half = self.outs[m].at[here.slot, pl.ds(0, PARTS // 2)]
+        remote(group, group, self.sx.at[m], self.rx.at[m, 0], here.across).wait_send()
+        remote(group, group, self.sy.at[m], self.ry.at[m, 0], here.beside).wait_send()
+        remote(half, half, self.dx.at[m], self.rd.at[m], here.across).wait_send()
+        remote(half, half, self.dy.at[m], self.rd.at[m], here.beside).wait_send()
+        four = self.outs[m].at[pl.ds(0, 4)]
+        both = remote(four, four, self.sc.at[m], self.rc.at[m], here.sibling)
+        both.wait_send()
+        both.wait_recv()
+
+
+def add_into(target, source):
+    rows, units = target.shape[:2]
+
+    def one(i, carry):
+        a, b = i // units, lax.rem(i, units)
+        target[a, b] = (target[a, b].astype(F32) + source[a, b].astype(F32)).astype(target.dtype)
+        return carry
+
+    lax.fori_loop(0, rows * units, one, 0)
+
+
+class Square:
+    @staticmethod
+    def scratch(units, tail, loaded):
+        held = [pltpu.VMEM((4, PARTS, units) + tail, BF16)] if loaded else []
+        half = pltpu.VMEM((PARTS // 2, units) + tail, BF16)
+        full = pltpu.VMEM((PARTS, units) + tail, BF16)
+        return held + [half, half, full, full, DMA((9,))]
+
+    def __init__(self, here, held, scratch, source=None):
+        self.here, self.held, self.source = here, held, source
+        self.corner_x, self.corner_y, self.side_x, self.side_y, self.sems = scratch
+
+    def load(self, start=True):
+        copy = pltpu.make_async_copy(self.source, self.held, self.sems.at[8])
+        copy.start() if start else copy.wait()
+
+    def move(self, n):
+        half, held, sems = PARTS // 2, self.held, self.sems
+        src = (held.at[3, pl.ds(0, half)], held.at[3, pl.ds(half, half)], held.at[1], held.at[2])[n]
+        dst = (self.corner_x, self.corner_y, self.side_x, self.side_y)[n]
+        peer = self.here.beside if n % 2 else self.here.across
+        return remote(src, dst, sems.at[2 * n], sems.at[2 * n + 1], peer)
+
+    def start(self):
+        if self.source is not None:
+            self.load(False)
+        for n in range(2):
+            self.move(n).start()
+
+    def sides(self):
+        half = PARTS // 2
+        self.move(0).wait_recv()
+        add_into(self.held.at[2, pl.ds(0, half)], self.corner_x)
+        self.move(3).start()
+        self.move(1).wait_recv()
+        add_into(self.held.at[1, pl.ds(half, half)], self.corner_y)
+        self.move(2).start()
+
+    def total(self, out):
+        self.move(2).wait_recv()
+        self.move(3).wait_recv()
+        units = out.shape[1]
+
+        def one(i, carry):
+            a, b = i // units, lax.rem(i, units)
+            value = self.held[0, a, b].astype(F32) + self.side_x[a, b].astype(F32) + self.side_y[a, b].astype(F32)
+            out[a, b] = value.astype(out.dtype)
+            return carry
+
+        lax.fori_loop(0, PARTS * units, one, 0)
+        for n in range(4):
+            self.move(n).wait_send()
+
+
+class Stack:
+    @staticmethod
+    def scratch(units, tail):
+        return [pltpu.VMEM((PARTS - 1, units) + tail, BF16), DMA((2, PARTS))]
+
+    def __init__(self, here, held, scratch):
+        self.here, self.held = here, held
+        self.arrived, self.sems = scratch
+
+    def moves(self):
+        for k in range(1, PARTS):
+            peer = self.here.along(k)
+            yield remote(self.held.at[peer[1]], self.arrived.at[k - 1], self.sems.at[0, k], self.sems.at[1, k], peer)
+
+    def start(self):
+        for move in self.moves():
+            move.start()
+
+    def finish(self, out):
+        for move in self.moves():
+            move.wait_recv()
+        units, z = out.shape[0], self.here.z
+
+        def one(unit, carry):
+            value = self.held[z, unit].astype(F32)
+            for k in range(PARTS - 1):
+                value += self.arrived[k, unit].astype(F32)
+            out[unit] = value
+            return carry
+
+        lax.fori_loop(0, units, one, 0)
+        for move in self.moves():
+            move.wait_send()
+
+
+class Cores:
+    @staticmethod
+    def scratch(units, tail):
+        return [pltpu.VMEM((4, PARTS, units) + tail, BF16), pltpu.VMEM((2, 8, PARTS) + tail, BF16), DMA((units,)), DMA((units,))]
+
+    def __init__(self, here, sums, scratch, hidden):
+        self.here, self.sums, self.hidden = here, sums, hidden
+        self.far, self.turn, self.send, self.recv = scratch
+
+    def moves(self, n, hidden):
+        here, slot = self.here, lax.rem(n, 2)
+        give = 1 - here.core
+        if hidden:
+            to = self.far.at[relative(here.square, n), :, pl.ds(0, self.hidden)]
+            return [(self.turn.at[slot, pl.ds(4 * give, 4)], to)], to
+        pairs = [(self.turn.at[slot, 2 * s + give], self.far.at[relative(here.square, s), :, n]) for s in range(4)]
+        return pairs, self.far.at[:, :, n]
+
+    def each(self, n, action):
+        if self.hidden:
+
+            @pl.when(n < self.hidden)
+            def _():
+                action(True)
+
+            @pl.when(n >= self.hidden)
+            def _():
+                action(False)
+        else:
+            action(False)
+
+    def waited(self, n, hidden, recv):
+        whole_ref = self.moves(n, hidden)[1]
+        move = remote(whole_ref, whole_ref, self.send.at[n], self.recv.at[n], self.here.sibling)
+        move.wait_recv() if recv else move.wait_send()
+
+    def put(self, n, value):
+        here, slot = self.here, lax.rem(n, 2)
+
+        @pl.when(n >= 2)
+        def _():
+            self.each(n - 2, lambda hidden: self.waited(n - 2, hidden, False))
+
+        self.turn[slot] = value.reshape(self.turn.shape[1:]).astype(BF16)
+
+        def action(hidden):
+            for src, dst in self.moves(n, hidden)[0]:
+                remote(src, dst, self.send.at[n], self.recv.at[n], here.sibling).start()
+            if hidden:
+                self.sums[relative(here.square, n), :, pl.ds(0, self.hidden)] = self.turn[slot, pl.ds(4 * here.core, 4)]
+            else:
+                for s in range(4):
+                    self.sums[relative(here.square, s), :, n] = self.turn[slot, 2 * s + here.core]
+
+        self.each(n, action)
+
+    def collect(self, n):
+        def action(hidden):
+            self.waited(n, hidden, True)
+            if hidden:
+                at = relative(self.here.square, n)
+                add_into(self.sums.at[at, :, pl.ds(0, self.hidden)], self.far.at[at, :, pl.ds(0, self.hidden)])
+            else:
+                for s in range(4):
+
+                    def one(a, carry):
+                        value = self.sums[s, a, n].astype(F32) + self.far[s, a, n].astype(F32)
+                        self.sums[s, a, n] = value.astype(BF16)
+                        return carry
+
+                    lax.fori_loop(0, PARTS, one, 0)
+
+        self.each(n, action)
+
+    def finish(self, count):
+        for n in (count - 2, count - 1):
+            self.waited(n, n < self.hidden, False)
+
+
+class Item:
+    def __init__(self, array, spec=None):
+        self.array = array
+        self.spec = spec or whole(array.shape)
+
+
+def anywhere(array):
+    return Item(array, pl.BlockSpec(memory_space=pl.ANY))
+
+
+def run(body, steps, ins, outs, scratch, collective, name, cost):
+    in_names, out_names, scratch_names = list(ins), list(outs), list(scratch)
+    flat_scratch, spans = [], {}
+    for key in scratch_names:
+        item = scratch[key]
+        many = isinstance(item, list)
+        spans[key] = (len(flat_scratch), len(item) if many else None)
+        flat_scratch += item if many else [item]
+
+    def kernel(*refs):
+        first, second = len(in_names), len(in_names) + len(out_names)
+        in_refs = dict(zip(in_names, refs[:first]))
+        out_refs = dict(zip(out_names, refs[first:second]))
+        rest = refs[second:]
+        own = {k: rest[at] if n is None else rest[at : at + n] for k, (at, n) in spans.items()}
+        here = Here()
+        step = pl.program_id(0)
+
+        @pl.when(step == 0)
+        def _():
+            here.greet()
+
+        body(here, step, in_refs, out_refs, own)
+
+    results = pl.pallas_call(
+        kernel,
+        grid=(steps,),
+        in_specs=[i.spec for i in ins.values()],
+        out_specs=tuple(o.spec for o in outs.values()),
+        out_shape=tuple(o.array for o in outs.values()),
+        scratch_shapes=flat_scratch,
+        compiler_params=pltpu.CompilerParams(
+            vmem_limit_bytes=BIG, collective_id=collective, has_side_effects=True, dimension_semantics=("arbitrary",)
+        ),
+        cost_estimate=pl.CostEstimate(flops=cost * 1150000000, bytes_accessed=0, transcendentals=0),
+        name=name,
+    )(*[i.array for i in ins.values()])
+    return dict(zip(out_names, results))
+
+
+def at_step(step, n):
+    def decorate(action):
+        pl.when(step == n)(action)
+
+    return decorate
+
+
+def first_kernel(here, step, ins, outs, own):
+    table = own["table"]
+    table[...] = jnp.zeros_like(table)
+    gain, shift, query_value = ins["gain"], ins["shift"], ins["query_value"]
+    for start, item in ((0, gain), (4, shift), (8, query_value)):
+        for i in range(4):
+            table[start + i : start + i + 1, :] = item[i // 2, i % 2 : i % 2 + 1, :].astype(F32)
+    table[12:14, :] = ins["output_bias"][...].astype(F32)
+    table[14:16, :] = ins["shrink_bias"][...].astype(F32)
+    table[16:17, :] = ins["decode_bias"][...].astype(F32)
+    fine = gain.shape[2]
+    wide = ins["expand_bias"][...].astype(F32)
+    for i in range(8):
+        table[17 + i : 18 + i, :] = wide[i // 4 : i // 4 + 1, fine * (i % 4) : fine * (i % 4 + 1)]
+    table[25:43, :] = ins["encode"][...].astype(F32).T
+    table[43:61, :] = ins["decode"][...].astype(F32)
+    names = ("project", "output", "expand", "shrink")
+    gather = Gather(
+        here, [table] + [ins[n].at[1] for n in names], [outs["table"]] + [outs[n] for n in names], own["gather"]
+    )
+    line = Line(here, [outs["signs"], outs["patches"]], own["line"])
+    keeps = [
+        pltpu.make_async_copy(ins[n].at[0], outs[n].at[0], own["keep"].at[i]) for i, n in enumerate(("signs", "patches"))
+    ]
+    messages = range(len(names) + 1)
+    gather.start(0)
+    for keep in keeps:
+        keep.start()
+    for m in messages[1:]:
+        gather.start(m)
+    for keep in keeps:
+        keep.wait()
+    line.start(0)
+    for k in range(1, PARTS):
+        line.hop(0, k)
+        for m in messages:
+            gather.hop(m, k)
+            gather.turn(m, k - 1)
+        if k == 1:
+            line.start(1)
+        else:
+            line.hop(1, k - 1)
+    for m in messages:
+        gather.turn(m, PARTS - 1)
+        gather.siblings(m)
+    line.hop(1, PARTS - 1)
+    for m in messages:
+        gather.corner(m)
+    for m in messages:
+        gather.finish(m)
+    for m in range(2):
+        line.finish(m)
+
+
+def forward_attention(coded, layer, slots, ins, extra, collective):
+    pieces, table, weight = ins["pieces"].array, ins["table"].array, ins["weight"].array
+    rows = pieces.shape[1]
+    width, triple = weight.shape
+    length = PARTS * rows
+    pairs, lanes = width // (2 * HD), 2 * HD
+    steps = PARTS + pairs
+    outs = {
+        "qkv": Item(shaped((length, triple)), pl.BlockSpec((rows, triple), lambda i: (jnp.minimum(i, PARTS - 1), 0))),
+        "normed": Item(shaped((rows, width))),
+        "mixed": Item(shaped((rows, width)), pl.BlockSpec((rows, lanes), lambda i: (0, jnp.maximum(i - PARTS, 0)))),
+        "logs": Item(shaped((rows, 128), F32)),
+    }
+    if coded:
+        outs["stream"] = Item(shaped((rows, width), F32))
+    scratch = {"qkv_held": pltpu.VMEM((length, triple), BF16)}
+    extra.declare(ins, outs, scratch)
+
+    def body(here, step, ins, outs, own):
+        extra.events(here, step, steps, ins, outs, own)
+        table = ins["table"]
+        held = own["qkv_held"]
+
+        @pl.when(step < PARTS)
+        def _():
+            if coded:
+                decode = table[43:61, :].astype(BF16)
+                stream = mm(ins["pieces"][step], decode) + table[16:17, :]
+            else:
+                stream = ins["pieces"][step].astype(F32)
+            hat, unused = norm_parts(stream)
+            normed = (hat * table[2 * layer : 2 * layer + 1, :] + table[4 + 2 * layer : 5 + 2 * layer, :]).astype(BF16)
+            at = pl.ds(pl.multiple_of(step * rows, rows), rows)
+            for part in range(3):
+                span = pl.ds(part * width, width)
+                value = mm(normed, ins["weight"][:, span])
+                if part != 1:
+                    shift = 8 + 2 * layer + part // 2
+                    value += table[shift : shift + 1, :]
+                value = value.astype(BF16)
+                outs["qkv"][:, span] = value
+                held[at, span] = value
+
+            @pl.when(step == 0)
+            def _():
+                outs["normed"][...] = normed
+                if coded:
+                    outs["stream"][...] = stream
+
+        @pl.when(step >= PARTS)
+        def _():
+            pair = step - PARTS
+            logs = outs["logs"]
+            lane = lax.broadcasted_iota(jnp.int32, (1, 128), 1)
+
+            @pl.when(pair == 0)
+            def _():
+                logs[...] = jnp.zeros_like(logs)
+
+            def span(part):
+                return pl.ds(pl.multiple_of(part * width + pair * lanes, lanes), lanes)
+
+            keys, values = held[:, span(1)], held[:, span(2)]
+            segments = ins["segment_row"][...]
+            for start in range(0, rows, BLOCK):
+                at = pl.ds(start, BLOCK)
+                same = ins["segment_column"][at, :] == segments
+                queries = held[at, span(0)] * jnp.asarray(HD**-0.5, BF16)
+                parts = []
+                for head in range(2):
+                    scores = jnp.where(same, mm(only(queries, head), keys, NT), masked_score)
+                    top = jnp.max(scores, axis=-1, keepdims=True)
+                    raised = jnp.exp(scores - top)
+                    total = jnp.sum(raised, axis=-1, keepdims=True)
+                    parts.append(mm(raised.astype(BF16), values) / total)
+                    logs[at, :] += jnp.where(lane == 2 * pair + head, top + jnp.log(total), 0.0)
+                outs["mixed"][at, :] = jnp.where(lanes_of(0), parts[0], parts[1]).astype(BF16)
+
+        extra.closing(here, step, steps, ins, outs, own)
+
+    return run(body, steps, ins, outs, scratch, collective, "forward_attention", 30)
+
+
+BLOCK = 128
+
+
+def middle_block(encoder, layer, slots, ins, extra, collective):
+    width = ins["output"].array.shape[1]
+    rows = ins["mixed"].array.shape[0]
+    hidden = ins["shrink"].array.shape[0]
+    fine = width // slots // PARTS
+    tile = 512
+    tiles = hidden // tile
+    feed = 2 * tiles if encoder else tiles
+    units = hidden // width + hidden // width + 1
+    wide = hidden // width
+    pairs, lanes = width // (2 * HD), 2 * HD
+    length = PARTS * rows
+    first_query = feed + units
+    first_key = first_query + pairs
+    steps = first_key + PARTS
+
+    def tiled(i):
+        return lax.rem(jnp.minimum(i, feed - 1), tiles)
+
+    late = feed - tiles
+    ins["expand"].spec = pl.BlockSpec((width, tile), lambda i: (0, tiled(i)))
+    ins["expand_shift"].spec = pl.BlockSpec((1, tile), lambda i: (0, tiled(i)))
+    ins["shrink"].spec = pl.BlockSpec((tile, width), lambda i: (tiled(i), 0))
+    ins["stream"].spec = pl.BlockSpec((1, rows, width), lambda i: (0, 0, 0))
+    outs = {
+        "query": Item(shaped((rows, width)), pl.BlockSpec((rows, lanes), lambda i: (0, jnp.clip(i - first_query, 0, pairs - 1)))),
+        "key": Item(shaped((rows, width))),
+        "value": Item(shaped((rows, width))),
+        "middle": Item(shaped((rows, width), F32)),
+        "small": Item(shaped((8, width), F32)),
+        "wide": Item(shaped((1, hidden), F32), pl.BlockSpec((1, tile), lambda i: (0, jnp.clip(i - late, 0, tiles - 1)))),
+    }
+    scratch = {
+        "active": pltpu.VMEM((rows, hidden), BF16),
+        "hidden_low": pltpu.VMEM((rows, hidden), BF16),
+        "normed": pltpu.VMEM((rows, width), BF16),
+        "hat": pltpu.VMEM((rows, width), F32),
+        "scale": pltpu.VMEM((rows, 1), F32),
+        "total": pltpu.VMEM((rows, width), F32),
+        "back": pltpu.VMEM((rows, width), F32),
+        "low": pltpu.VMEM((rows, width), BF16),
+        "branch": pltpu.VMEM((rows, width), BF16),
+        "delta": pltpu.VMEM((rows, 128), F32),
+        "qkv_held": pltpu.VMEM((length, 3 * width), BF16),
+        "qkv_sem": DMA((1,)),
+        "mixed_back": pltpu.VMEM((PARTS, rows, width), BF16),
+        "stats": pltpu.VMEM((PARTS, 32, rows), F32),
+        "line": Line.scratch(2),
+        "cores": Cores.scratch(units, (fine, width)),
+    }
+    if encoder:
+        outs["code_grad"] = Item(shaped((CODE, width), F32))
+        scratch["slope"] = pltpu.VMEM((tiles, rows, tile), BF16)
+        scratch["sums"] = pltpu.VMEM((4, PARTS, units, fine, width), BF16)
+    else:
+        outs["decoded"] = Item(shaped((rows, width)))
+        outs["sums"] = Item(shaped((4, PARTS, units, fine, width)))
+    extra.declare(ins, outs, scratch)
+    extra.marks = {"feed": feed, "grads": feed, "query": first_query, "key": first_key}
+
+    def body(here, step, ins, outs, own):
+        table = ins["table"]
+        normed, hat, scale, total, back, low = (own[n] for n in ("normed", "hat", "scale", "total", "back", "low"))
+        mixed_back, stats, held = own["mixed_back"], own["stats"], own["qkv_held"]
+        sums = own["sums"] if encoder else outs["sums"]
+        cores = Cores(here, sums, own["cores"], wide)
+        line = Line(here, [mixed_back, stats], own["line"])
+        load = pltpu.make_async_copy(ins["qkv"], held, own["qkv_sem"].at[0])
+        gain, shift = table[2 * layer + 1 : 2 * layer + 2, :], table[5 + 2 * layer : 6 + 2 * layer, :]
+        extra.events(here, step, steps, ins, outs, own)
+
+        @at_step(step, 0)
+        def _():
+            load.start()
+            middle = ins["stream"][0].astype(F32) + mm(ins["mixed"][...], ins["output"][...]) + table[12 + layer : 13 + layer, :]
+            hat[...], scale[...] = norm_parts(middle)
+            normed[...] = (hat[...] * gain + shift).astype(BF16)
+            total[...] = middle + table[14 + layer : 15 + layer, :]
+            back[...] = jnp.zeros_like(back)
+            if not encoder:
+                low[...] = ins["other"][...]
+
+        def columns_at(n):
+            return pl.ds(pl.multiple_of(n * tile, tile), tile)
+
+        def forward(n):
+            value = mm(normed[...], ins["expand"][...]) + ins["expand_shift"][...]
+            active, steep = gelu_parts(value)
+            active = active.astype(BF16)
+            own["active"][:, columns_at(n)] = active
+            total[...] += mm(active, ins["shrink"][...])
+            return steep
+
+        def backward(n, steep):
+            hidden_low = (steep * mm(low[...], ins["shrink"][...], NT)).astype(BF16)
+            own["hidden_low"][:, columns_at(n)] = hidden_low
+            outs["wide"][...] = columns(hidden_low.astype(F32))
+            back[...] += mm(hidden_low, ins["expand"][...], NT)
+
+        if encoder:
+
+            @pl.when(step < tiles)
+            def _():
+                own["slope"][step] = forward(step).astype(BF16)
+
+            @at_step(step, tiles - 1)
+            def _():
+                code = table[25:43, :].astype(BF16)
+                encoded_low = total[...].astype(BF16)
+                coded = mm(encoded_low, code, NT)
+                size = lax.rsqrt(jnp.sum(coded * coded, axis=-1, keepdims=True) + epsilon)
+                unit = coded * size
+                grad = ins["other"][...]
+                coded_low = ((grad - unit * jnp.sum(unit * grad, axis=-1, keepdims=True)) * size).astype(BF16)
+                outs["code_grad"][...] = mm(coded_low, encoded_low, TN)
+                total[...] = mm(coded_low, code)
+                low[...] = total[...].astype(BF16)
+
+            @pl.when((step >= tiles) & (step < feed))
+            def _():
+                backward(step - tiles, own["slope"][step - tiles].astype(F32))
+        else:
+
+            @pl.when(step < tiles)
+            def _():
+                backward(step, forward(step))
+
+        @at_step(step, feed - 1)
+        def _():
+            if encoder:
+                grad_out = total[...]
+            else:
+                outs["decoded"][...] = total[...].astype(BF16)
+                grad_out = low[...].astype(F32)
+            grad = back[...]
+            middle = grad_out + norm_back(grad, gain, hat[...], scale[...])
+            outs["middle"][...] = middle
+            branch = middle.astype(BF16)
+            own["branch"][...] = branch
+            mixed_low = mm(branch, ins["output"][...], NT).astype(BF16)
+            mixed_back[0] = mixed_low
+            product = mixed_low.astype(F32) * ins["mixed"][...].astype(F32)
+            feature = lax.broadcasted_iota(jnp.int32, (width, 128), 0) // HD
+            heads = (feature == lax.broadcasted_iota(jnp.int32, (width, 128), 1)).astype(F32)
+            delta = lax.dot_general(product, heads, NN, preferred_element_type=F32, precision=lax.Precision.HIGHEST)
+            own["delta"][...] = delta
+            stats[0, pl.ds(0, 16)] = ins["logs"][...].T[:16]
+            stats[0, pl.ds(16, 16)] = delta.T[:16]
+            for m in range(2):
+                line.start(m)
+            outs["small"][...] = jnp.concatenate(
+                [columns(grad * hat[...]), columns(grad), columns(branch.astype(F32)), columns(low[...].astype(F32))]
+                + [jnp.zeros_like(columns(grad))] * 4
+            )
+
+        unit = step - feed
+
+        def wide_at(n):
+            return pl.ds(pl.multiple_of(n * width, width), width)
+
+        @pl.when((unit >= 0) & (unit < wide))
+        def _():
+            cores.put(unit, mm(own["active"][:, wide_at(unit)], low[...], TN))
+
+        @pl.when((unit >= wide) & (unit < 2 * wide))
+        def _():
+            cores.put(unit, mm(normed[...], own["hidden_low"][:, wide_at(unit - wide)], TN))
+
+        @pl.when(unit == 2 * wide)
+        def _():
+            cores.put(unit, mm(ins["mixed"][...], own["branch"][...], TN))
+
+        @pl.when((unit >= 2) & (unit < units))
+        def _():
+            cores.collect(unit - 2)
+
+        @pl.when(unit == units)
+        def _():
+            cores.collect(unit - 2)
+            cores.collect(unit - 1)
+            cores.finish(units)
+
+        for n, k in ((units - 1, 1), (units + 3, 2)):
+
+            @pl.when(unit == n)
+            def _():
+                for m in range(2):
+                    line.hop(m, k)
+
+        @at_step(step, first_query)
+        def _():
+            load.wait()
+
+        eighth = jnp.asarray(HD**-0.5, BF16)
+
+        @pl.when((step >= first_query) & (step < first_key))
+        def _():
+            pair = step - first_query
+            lane = lax.broadcasted_iota(jnp.int32, (1, 128), 1)
+
+            def span(part):
+                return pl.ds(pl.multiple_of(part * width + pair * lanes, lanes), lanes)
+
+            keys, values = held[:, span(1)], held[:, span(2)]
+            segments = ins["segment_row"][...]
+            for start in range(0, rows, BLOCK):
+                at = pl.ds(start, BLOCK)
+                same = ins["segment_column"][at, :] == segments
+                queries = held[at, span(0)] * eighth
+                grads = mixed_back[0, at, span(0)]
+                parts = []
+                for head in range(2):
+                    mine = lane == 2 * pair + head
+                    log_sum = jnp.sum(jnp.where(mine, ins["logs"][at, :], 0.0), axis=-1, keepdims=True)
+                    centre = jnp.sum(jnp.where(mine, own["delta"][at, :], 0.0), axis=-1, keepdims=True)
+                    scores = jnp.where(same, mm(only(queries, head), keys, NT), masked_score)
+                    probability = jnp.exp(scores - log_sum)
+                    prob_grad = mm(only(grads, head), values, NT)
+                    score_low = (probability * (prob_grad - centre)).astype(BF16)
+                    parts.append(mm(score_low, keys) * HD**-0.5)
+                outs["query"][at, :] = jnp.where(lanes_of(0), parts[0], parts[1]).astype(BF16)
+
+        piece = step - first_key
+
+        @pl.when(piece == 2)
+        def _():
+            for m in range(2):
+                line.hop(m, 3)
+
+        @pl.when(piece >= 0)
+        def _():
+            of_piece = pl.ds(pl.multiple_of(piece * rows, rows), rows)
+            segments = ins["segment_row"][:, of_piece]
+
+            def one(pair, carry):
+                def span(part):
+                    return pl.ds(pl.multiple_of(part * width + pair * lanes, lanes), lanes)
+
+                queries = held[of_piece, span(0)]
+                grads = mixed_back[piece, :, span(0)]
+                for start in range(0, rows, BLOCK):
+                    at = pl.ds(start, BLOCK)
+                    same = ins["segment_column"][at, :] == segments
+                    keys = held[at, span(1)] * eighth
+                    values = held[at, span(2)]
+                    key_parts, value_parts = [], []
+                    for head in range(2):
+                        log_sum = stats[piece, pl.ds(2 * pair + head, 1), :]
+                        centre = stats[piece, pl.ds(16 + 2 * pair + head, 1), :]
+                        scores = jnp.where(same, mm(only(keys, head), queries, NT), masked_score)
+                        probability = jnp.exp(scores - log_sum)
+                        value_parts.append(mm(probability.astype(BF16), grads))
+                        prob_grad = mm(only(values, head), grads, NT)
+                        score_low = (probability * (prob_grad - centre)).astype(BF16)
+                        key_parts.append(mm(score_low, queries) * HD**-0.5)
+                    key_part = jnp.where(lanes_of(0), key_parts[0], key_parts[1])
+                    value_part = jnp.where(lanes_of(0), value_parts[0], value_parts[1])
+
+                    @pl.when(piece == 0)
+                    def _():
+                        hat[at, span(0)] = key_part
+                        total[at, span(0)] = value_part
+
+                    @pl.when(piece > 0)
+                    def _():
+                        hat[at, span(0)] += key_part
+                        total[at, span(0)] += value_part
+
+                return carry
+
+            lax.fori_loop(0, pairs, one, 0)
+
+        @pl.when(piece == PARTS - 1)
+        def _():
+            outs["key"][...] = hat[...].astype(BF16)
+            outs["value"][...] = total[...].astype(BF16)
+            for m in range(2):
+                line.finish(m)
+
+        extra.closing(here, step, steps, ins, outs, own)
+
+    return run(body, steps, ins, outs, scratch, collective, "encoder_middle" if encoder else "decoder_middle", 80)
+
+
+def projection_back(coded, layer, slots, ins, extra, collective):
+    rows, width = ins["query"].array.shape
+    fine = width // slots // PARTS
+    units = 3
+    steps = 1 + units
+    ins["stream"].spec = pl.BlockSpec((1, rows, width), lambda i: (0, 0, 0))
+    outs = {"small": Item(shaped((8, width), F32)), "sums": Item(shaped((4, PARTS, units, fine, width)))}
+    if coded:
+        outs["unit_grad"] = Item(shaped((rows, CODE), F32))
+        outs["decode_grad"] = Item(shaped((CODE, width), F32))
+        ins["pieces"].spec = pl.BlockSpec((1, rows, CODE), lambda i: (0, 0, 0))
+    else:
+        outs["grad"] = Item(shaped((rows, width), F32))
+    scratch = {"cores": Cores.scratch(units, (fine, width))}
+    extra.declare(ins, outs, scratch)
+
+    def body(here, step, ins, outs, own):
+        table = ins["table"]
+        cores = Cores(here, outs["sums"], own["cores"], 0)
+        extra.events(here, step, steps, ins, outs, own)
+        sources = (ins["query"], ins["key"], ins["value"])
+        for n in range(units):
+
+            @at_step(step, n)
+            def _():
+                cores.put(jnp.int32(n), mm(ins["normed"][...], sources[n][...], TN))
+
+        @at_step(step, units)
+        def _():
+            query, key, value = sources
+            weight = ins["weight"]
+            grad = mm(query[...], weight[:, :width], NT)
+            grad += mm(key[...], weight[:, width : 2 * width], NT)
+            grad += mm(value[...], weight[:, 2 * width :], NT)
+            hat, scale = norm_parts(ins["stream"][0].astype(F32))
+            start = ins["middle"][...] + norm_back(grad, table[2 * layer : 2 * layer + 1, :], hat, scale)
+            small = [columns(grad * hat), columns(grad), columns(query[...].astype(F32)), columns(value[...].astype(F32))]
+            if coded:
+                start_low = start.astype(BF16)
+                outs["unit_grad"][...] = mm(start_low, table[43:61, :].astype(BF16), NT)
+                outs["decode_grad"][...] = mm(ins["pieces"][0], start_low, TN)
+                small.append(columns(start_low.astype(F32)))
+            else:
+                outs["grad"][...] = start
+            small += [jnp.zeros_like(small[0])] * (8 - len(small))
+            outs["small"][...] = jnp.concatenate(small)
+            for n in range(units):
+                cores.collect(jnp.int32(n))
+            cores.finish(units)
+
+        extra.closing(here, step, steps, ins, outs, own)
+
+    return run(body, steps, ins, outs, scratch, collective, "projection_back", 12)
+
+
+def last_kernel(here, step, ins, outs, own):
+    square = Square(here, own["square"][0], own["square"][1:], ins["sums"])
+    stack = Stack(here, own["total"], own["stack"])
+    tables, arrived, sems = own["tables"], own["arrived"], own["sems"]
+    square.load()
+    in0, in1, mid0, mid1 = (ins[n] for n in ("in0", "in1", "mid0", "mid1"))
+    rows = [in0[0:1], mid0[0:1], in1[0:1], mid1[0:1], in0[1:2], mid0[1:2], in1[1:2], mid1[1:2]]
+    rows += [in0[2:4], in1[2:4], mid0[2:3], mid1[2:3], mid0[3:4], mid1[3:4], in1[4:5]]
+    at = 0
+    tables[0] = jnp.zeros_like(tables[0])
+    for value in rows:
+        tables[0, at : at + value.shape[0], :] = value
+        at += value.shape[0]
+    width = tables.shape[2]
+    for wide in (ins["wide0"], ins["wide1"]):
+        for start in range(0, wide.shape[1], width):
+            tables[0, at : at + 1, :] = wide[:, start : start + width]
+            at += 1
+    for value in (ins["code_grad"], ins["decode_grad"]):
+        tables[0, at : at + value.shape[0], :] = value[...]
+        at += value.shape[0]
+
+    def move(stage, peer, k=0):
+        slot = stage + k
+        return remote(tables.at[stage], arrived.at[slot], sems.at[0, slot], sems.at[1, slot], peer)
+
+    peers = (here.sibling, here.across, here.beside)
+    move(0, peers[0]).start()
+    square.start()
+
+    def meet(stage):
+        move(stage, peers[stage]).wait_recv()
+        tables[stage + 1] = tables[stage] + arrived[stage]
+        if stage + 1 < len(peers):
+            move(stage + 1, peers[stage + 1]).start()
+
+    meet(0)
+    square.sides()
+    meet(1)
+    square.total(own["total"])
+    stack.start()
+    meet(2)
+    for k in range(1, PARTS):
+        move(3, here.along(k), k - 1).start()
+    stack.finish(outs["units"])
+    value = tables[3]
+    for k in range(1, PARTS):
+        move(3, here.along(k), k - 1).wait_recv()
+        value += arrived[2 + k]
+    outs["table"][...] = value
+    for stage, peer in enumerate(peers):
+        move(stage, peer).wait_send()
+    for k in range(1, PARTS):
+        move(3, here.along(k), k - 1).wait_send()
+
+
+class Nothing:
+    def declare(self, ins, outs, scratch):
+        pass
+
+    def events(self, here, step, steps, ins, outs, own):
+        pass
+
+    def closing(self, here, step, steps, ins, outs, own):
+        pass
+
+
+class Beside(Nothing):
+    def __init__(self, slots, gathers=None, gather_steps=(), squares=None, square_steps=None, stacks=None, stack_steps=None, inner=None):
+        self.slots, self.gathers, self.gather_steps = slots, gathers or {}, gather_steps
+        self.squares, self.square_steps = squares or {}, square_steps or {}
+        self.stacks, self.stack_steps = stacks or {}, stack_steps or {}
+        self.inner = inner
+
+    def declare(self, ins, outs, scratch):
+        for name, (array, layer) in self.gathers.items():
+            ins["shard_" + name] = anywhere(array)
+            outs["gathered_" + name] = anywhere(shaped((self.slots, PARTS) + array.shape[1:]))
+        if self.gathers:
+            scratch["gather"] = Gather.scratch(len(self.gathers))
+        for name, (sums, first, units) in self.squares.items():
+            ins["square_" + name] = anywhere(sums)
+            tail = sums.shape[3:]
+            outs["total_" + name] = Item(shaped((PARTS, units) + tail))
+            scratch["square_" + name] = Square.scratch(units, tail, True)
+        for name, array in self.stacks.items():
+            ins["stack_" + name] = Item(array)
+            outs["stacked_" + name] = Item(shaped(array.shape[1:], F32))
+            scratch["stack_" + name] = Stack.scratch(array.shape[1], array.shape[2:])
+        if self.inner:
+            name, units = self.inner
+            shape = scratch["sums"].shape
+            outs["total_" + name] = Item(shaped(shape[1:]))
+            scratch["inner"] = Square.scratch(units, shape[3:], False)
+
+    def events(self, here, step, steps, ins, outs, own):
+        if self.gathers:
+            names = list(self.gathers)
+            sources = [ins["shard_" + n].at[self.gathers[n][1]] for n in names]
+            gather = Gather(here, sources, [outs["gathered_" + n] for n in names], own["gather"])
+            count = range(len(names))
+
+            def each(*actions):
+                for action, *more in actions:
+                    for m in count:
+                        action(m, *more)
+
+            start, one, two, three, turn, corner = self.gather_steps
+            stages = [
+                (start, [(gather.start,)]),
+                (one, [(gather.hop, 1), (gather.turn, 0)]),
+                (two, [(gather.hop, 2), (gather.turn, 1)]),
+                (three, [(gather.hop, 3), (gather.turn, 2)]),
+                (turn, [(gather.turn, 3), (gather.siblings,)]),
+                (corner, [(gather.corner,)]),
+                (steps - 1, [(gather.finish,)]),
+            ]
+            for n, actions in stages:
+                at_step(step, n)(lambda actions=actions: each(*actions))
+        for name, (sums, first, units) in self.squares.items():
+            scratch = own["square_" + name]
+            square = Square(here, scratch[0], scratch[1:], ins["square_" + name].at[:, :, pl.ds(first, units)])
+            load, start, sides, total = self.square_steps[name]
+            at_step(step, load)(square.load)
+            at_step(step, start)(square.start)
+            at_step(step, sides)(square.sides)
+            at_step(step, total)(lambda square=square, name=name: square.total(outs["total_" + name]))
+        for name in self.stacks:
+            stack = Stack(here, ins["stack_" + name], own["stack_" + name])
+            start, finish = self.stack_steps[name]
+            at_step(step, start)(stack.start)
+            at_step(step, finish)(lambda stack=stack, name=name: stack.finish(outs["stacked_" + name]))
+        if self.inner:
+            name, units = self.inner
+            square = Square(here, own["sums"], own["inner"])
+            start, sides = self.square_steps[name]
+            at_step(step, start)(square.start)
+            at_step(step, sides)(square.sides)
+
+    def closing(self, here, step, steps, ins, outs, own):
+        if self.inner:
+            name, units = self.inner
+            square = Square(here, own["sums"], own["inner"])
+            at_step(step, steps - 1)(lambda: square.total(outs["total_" + name]))
+
+
+def on_device(
+    patches,
+    segments,
+    code_bits,
+    norm_gain,
+    norm_shift,
+    project_weight,
+    query_value_bias,
+    output_weight,
+    output_bias,
+    expand_weight,
+    expand_bias,
+    shrink_weight,
+    shrink_bias,
+    encode_weight,
+    decode_weight,
+    decode_bias,
+    cotangent,
+):
+    slots, parts = lax.axis_size("slot"), lax.axis_size("seq")
+    fine, width = project_weight.shape[1], patches.shape[-1]
+    if slots != 8 or parts != PARTS or fine % 8:
+        return plain_device(
+            patches,
+            segments,
+            code_bits,
+            norm_gain,
+            norm_shift,
+            project_weight,
+            query_value_bias,
+            output_weight,
+            output_bias,
+            expand_weight,
+            expand_bias,
+            shrink_weight,
+            shrink_bias,
+            encode_weight,
+            decode_weight,
+            decode_bias,
+            cotangent,
+        )
+    slot, z = lax.axis_index("slot"), lax.axis_index("seq")
+    devices, rows, hidden = slots * parts, patches.shape[1], expand_weight.shape[-1]
+    signs = ((2 * code_bits - 1).astype(F32) * CODE ** (-0.5)).astype(BF16)
+
+    ins = {
+        "gain": Item(norm_gain),
+        "shift": Item(norm_shift),
+        "query_value": Item(query_value_bias),
+        "output_bias": Item(output_bias),
+        "shrink_bias": Item(shrink_bias),
+        "decode_bias": Item(decode_bias.reshape(1, fine)),
+        "expand_bias": Item(expand_bias),
+        "encode": Item(encode_weight),
+        "decode": Item(decode_weight),
+    }
+    weights = {"project": project_weight, "output": output_weight, "expand": expand_weight, "shrink": shrink_weight}
+    for name, array in (("signs", signs), ("patches", patches), *weights.items()):
+        ins[name] = anywhere(array)
+    outs = {
+        "table": anywhere(shaped((slots, parts, 64, fine), F32)),
+        "signs": anywhere(shaped((parts, rows, CODE))),
+        "patches": anywhere(shaped((parts, rows, width))),
+    }
+    for name, array in weights.items():
+        outs[name] = anywhere(shaped((slots, parts) + array.shape[1:]))
+    scratch = {
+        "table": pltpu.VMEM((64, fine), F32),
+        "gather": Gather.scratch(5),
+        "line": Line.scratch(2),
+        "keep": DMA((2,)),
+    }
+    first = run(first_kernel, 1, ins, outs, scratch, 0, "first_gather", 70)
+
+    small = first["table"].reshape(devices, 64, fine)
+    table = small.transpose(1, 0, 2).reshape(64, width)
+    expand_shifts = small[:, 17:25].reshape(devices, 2, 4, fine).transpose(1, 0, 2, 3).reshape(2, 1, hidden)
+    around = jnp.arange(parts) ^ z
+    pieces = segments[0].reshape(parts, rows)[around]
+    segment_row = pieces.reshape(1, parts * rows)
+    segment_column = pieces[0].reshape(rows, 1)
+
+    def flat(array):
+        return array.reshape(-1, array.shape[-1])
+
+    def forward(layer, pieces, weight, extra, collective):
+        ins = {
+            "pieces": Item(pieces),
+            "table": Item(table),
+            "weight": Item(weight),
+            "segment_row": Item(segment_row),
+            "segment_column": Item(segment_column),
+        }
+        return forward_attention(layer == 1, layer, slots, ins, extra, collective)
+
+    def middle(layer, stream, other, ahead, weights, extra, collective):
+        ins = {
+            "stream": Item(stream),
+            "mixed": Item(ahead["mixed"]),
+            "other": Item(other),
+            "logs": Item(ahead["logs"]),
+            "qkv": anywhere(ahead["qkv"]),
+            "table": Item(table),
+            "output": Item(weights["output"]),
+            "expand": Item(weights["expand"]),
+            "expand_shift": Item(expand_shifts[layer]),
+            "shrink": Item(weights["shrink"]),
+            "segment_row": Item(segment_row),
+            "segment_column": Item(segment_column),
+        }
+        return middle_block(layer == 0, layer, slots, ins, extra, collective)
+
+    def projection(layer, stream, ahead, between, weight, extra, collective, **more):
+        ins = {
+            "query": Item(between["query"]),
+            "key": Item(between["key"]),
+            "value": Item(between["value"]),
+            "normed": Item(ahead["normed"]),
+            "stream": Item(stream),
+            "middle": Item(between["middle"]),
+            "table": Item(table),
+            "weight": Item(weight),
+        }
+        ins.update({k: Item(v) for k, v in more.items()})
+        return projection_back(layer == 1, layer, slots, ins, extra, collective)
+
+    decoder = {n: flat(first[n]) for n in weights}
+    beside = Beside(slots, {n: (weights[n], 0) for n in ("project", "output")}, (0, 2, 4, 5, 7, 8))
+    ahead1 = forward(1, first["signs"], decoder["project"], beside, 1)
+    encoder = {n: flat(ahead1["gathered_" + n]) for n in ("project", "output")}
+
+    beside = Beside(slots, {n: (weights[n], 0) for n in ("expand", "shrink")}, (0, 3, 6, 9, 14, 18))
+    stream1 = ahead1["stream"][None]
+    between1 = middle(1, stream1, cotangent[0], ahead1, decoder, beside, 2)
+    encoder.update({n: flat(between1["gathered_" + n]) for n in ("expand", "shrink")})
+    after1 = projection(1, stream1, ahead1, between1, decoder["project"], Nothing(), 3, pieces=first["signs"])
+
+    beside = Beside(
+        slots,
+        squares={"one": (after1["sums"], 0, 3), "two": (between1["sums"], 0, 4)},
+        square_steps={"one": (0, 1, 3, 6), "two": (0, 1, 4, 9)},
+    )
+    ahead0 = forward(0, first["patches"], encoder["project"], beside, 4)
+    beside = Beside(
+        slots,
+        squares={"three": (between1["sums"], 4, 5)},
+        square_steps={"three": (0, 1, 5, 12), "inner": (22, 26)},
+        stacks={n: ahead0["total_" + n] for n in ("one", "two")},
+        stack_steps={"one": (0, 8), "two": (2, 10)},
+        inner=("inner", 9),
+    )
+    between0 = middle(0, first["patches"], after1["unit_grad"], ahead0, encoder, beside, 5)
+    beside = Beside(
+        slots,
+        stacks={"three": between0["total_three"], "inner": between0["total_inner"]},
+        stack_steps={"three": (0, 3), "inner": (0, 3)},
+    )
+    after0 = projection(0, first["patches"], ahead0, between0, encoder["project"], beside, 6)
+
+    ins = {
+        "sums": anywhere(after0["sums"]),
+        "in0": Item(after0["small"]),
+        "in1": Item(after1["small"]),
+        "mid0": Item(between0["small"]),
+        "mid1": Item(between1["small"]),
+        "wide0": Item(between0["wide"]),
+        "wide1": Item(between1["wide"]),
+        "code_grad": Item(between0["code_grad"]),
+        "decode_grad": Item(after1["decode_grad"]),
+    }
+    outs = {"units": Item(shaped((3, fine, width), F32)), "table": Item(shaped((64, width), F32))}
+    scratch = {
+        "square": Square.scratch(3, (fine, width), True),
+        "total": pltpu.VMEM((parts, 3, fine, width), BF16),
+        "stack": Stack.scratch(3, (fine, width)),
+        "tables": pltpu.VMEM((4, 64, width), F32),
+        "arrived": pltpu.VMEM((6, 64, width), F32),
+        "sems": DMA((2, 6)),
+    }
+    last = run(last_kernel, 1, ins, outs, scratch, 7, "last_sums", 30)
+
+    device = slot * parts + z
+    mine = lax.dynamic_slice(last["table"], (0, device * fine), (64, fine))
+    wide = last["table"][17:25].reshape(2, hidden)
+    wide = lax.dynamic_slice(wide, (0, device * (hidden // devices)), (2, hidden // devices))
+    decoder_mlp = jnp.concatenate([between0["stacked_two"], after0["stacked_three"]])
+    encoder_mlp, encoder_project, decoder_project = after0["stacked_inner"], last["units"], between0["stacked_one"]
+
+    def both(cut):
+        return jnp.stack([cut(encoder_mlp), cut(decoder_mlp)])
+
+    def joined(units):
+        return units.transpose(1, 0, 2).reshape(fine, units.shape[0] * width)
+
+    return (
+        between1["decoded"][None],
+        after0["grad"][None],
+        mine[0:4].reshape(2, 2, fine),
+        mine[4:8].reshape(2, 2, fine),
+        jnp.stack([joined(encoder_project), joined(decoder_project)]),
+        mine[8:12].reshape(2, 2, fine),
+        both(lambda g: g[8]),
+        mine[12:14],
+        both(lambda g: joined(g[4:8])),
+        wide,
+        both(lambda g: g[0:4].reshape(4 * fine, width)),
+        mine[14:16],
+        mine[25:43].T,
+        mine[43:61],
+        mine[16],
+    )
+
+
+def plain_norm(stream, gains, shifts):
     centre = stream - jnp.mean(stream, axis=-1, keepdims=True)
     spread = jnp.mean(centre * centre, axis=-1, keepdims=True)
     return centre * lax.rsqrt(spread + epsilon) * gains + shifts
@@ -68,7 +1422,7 @@
     slot_count, row_count, model_width = stream.shape
     seq_parts = lax.axis_size("seq")
     head_width = model_width // seq_parts
-    normed = layer_norm(stream, gains[0].astype(jnp.float32), shifts[0].astype(jnp.float32)).astype(
+    normed = plain_norm(stream, gains[0].astype(jnp.float32), shifts[0].astype(jnp.float32)).astype(
         jnp.bfloat16
     )
     bias_row = jnp.concatenate(
@@ -118,7 +1472,7 @@
         + jnp.dot(mixed_rows, output, preferred_element_type=jnp.float32)
         + output_shift.astype(jnp.float32)
     )
-    normed_mid = layer_norm(
+    normed_mid = plain_norm(
         middle, gains[1].astype(jnp.float32), shifts[1].astype(jnp.float32)
     ).astype(jnp.bfloat16)
     hidden = jnp.dot(normed_mid, expand, preferred_element_type=jnp.float32) + expand_shift.astype(
@@ -178,7 +1532,7 @@
         "stf,if->sti", hidden_low, expand, preferred_element_type=jnp.float32
     )
     unused, norm_back = jax.vjp(
-        layer_norm, middle, gains[1].astype(jnp.float32), shifts[1].astype(jnp.float32)
+        plain_norm, middle, gains[1].astype(jnp.float32), shifts[1].astype(jnp.float32)
     )
     middle_part, gain_mid_grad, shift_mid_grad = norm_back(normed_mid_grad)
     middle_grad = grad_out + middle_part
@@ -250,7 +1604,7 @@
         "stj,ij->sti", project_low, project, preferred_element_type=jnp.float32
     )
     unused, norm_back = jax.vjp(
-        layer_norm, stream, gains[0].astype(jnp.float32), shifts[0].astype(jnp.float32)
+        plain_norm, stream, gains[0].astype(jnp.float32), shifts[0].astype(jnp.float32)
     )
     stream_part, gain_in_grad, shift_in_grad = norm_back(normed_grad)
     input_part = middle_grad + stream_part
@@ -269,7 +1623,7 @@
     return (input_part, grads)
 
 
-def on_device(
+def plain_device(
     patches,
     segments,
     code_bits,

time: 2230 us -> 624 us (0.28)
  waiting for transfers between devices: 1010 us -> 0 us
  blocking collectives: 614 us -> 0 us
  Pallas kernels: 0 us -> 587 us
  matrix products: 252 us -> 0 us
  other arithmetic: 161 us -> 4.66 us
  local copies, waits for them, and re-layouts: 125 us -> 22.5 us
  starting transfers between devices: 36.9 us -> 0 us
    reduce_scatter x4 -> x0, waiting for transfers between devices: 706 us -> none  [the longest x1 212 us: on_device(): lax.psum_scatter(pairs[6], ('slot', 'seq'), scatter_dimension=1, tiled=True)]
    pallas_call x0 -> x8, Pallas kernels: none -> 587 us  [run(): pl.pallas_call(kernel, grid=(steps,), in_specs=[i.spec for i in ins.value...]
    all_gather x8 -> x0, blocking collectives: 577 us -> none  [the longest x1 100 us: gather_weights(): lax.all_gather(shards[10], ('slot', 'seq'), axis=0, tiled=True)]
    dot_general x66 -> x0, matrix products: 252 us -> none  [the longest x6 32.1 us: backward_block(): jnp.einsum('sqhd,skhd->shqk', out_grad, values, preferred_element_type=jn...]
    unnamed x14 -> x0, waiting for transfers between devices: 175 us -> none
    all_to_all x8 -> x0, waiting for transfers between devices: 130 us -> none  [the longest x2 103 us: backward_block(): lax.all_to_all(joined, 'seq', split_axis=1, concat_axis=3, tiled=True)]
    another operation x14 -> x4, other arithmetic: 48.4 us -> 3.18 us  [the longest x3 2.39 us: both(): return jnp.stack([cut(encoder_mlp), cut(decoder_mlp)])]
    unnamed x362 -> x13, local copies, waits for them, and re-layouts: 41.8 us -> 3.23 us
  transfers between devices with their start and end apart: 19 -> 0, of which waited for: 11 -> 0; matrix products, arithmetic and copies ran while one was open for 14% -> 0% of each run, Pallas kernels for 0% -> 0%
where the time goes in v1:
time: 624 us; the launch traced here: 615 us
  Pallas kernels  587 us (94%)
  local copies, waits for them, and re-layouts  22.5 us (4%)
    pallas_call x8, Pallas kernels, run(): pl.pallas_call(kernel, grid=(steps,), in_specs=[i.spec for i in ins.value...  587 us

profile of v1, /device:TPU:0, one launch (start us, length us, event | category | flops | bytes accessed | tf_op | source)
XLA Modules:
  0.0 615.2 jit_solution(9683257859721410920)
XLA Ops:
  0.7 0.7 reduce
  2.6 0.8 fusion.3
  3.3 0.8 copy.62.refs_9_
  4.1 0.8 copy.65.refs_4_.refs_11_
  4.9 100.8 %first_gather.1 = (f32[8,4,64,24]{3,2,1,0:T(8,128)}, bf16[4,384,18]{2,1,0:T(8,128)(2,1)}, bf16[4,384,768]{2,1,0:T(8,128)(2,1)}, bf16[8,4,24,2304]{3,2,1,0:T(8,12...) custom-call(bf16[2,2,24]{2,1,0:T(2,128)(2,1)} %refs_0_.1, ...), custom_call_target="tpu_custom_call" | custom-call | flops 80499998720 | tf_op jit(solution)/shard_map/first_gather/pallas_call | solution.py:507
  105.8 1.0 slice.77
  106.7 1.5 copy.63
  108.4 0.8 copy.64.refs_1_.refs_5_.refs_6_
  109.3 0.7 squeeze.14.refs_8_
  110.2 0.7 squeeze.13.refs_8_
  110.9 40.7 %forward_attention.2 = (bf16[1536,2304]{1,0:T(8,128)(2,1)}, bf16[384,768]{1,0:T(8,128)(2,1)}, bf16[384,768]{1,0:T(8,128)(2,1)}, f32[384,128]{1,0:T(8,128)}, f32[...) custom-call(bf16[4,384,18]{2,1,0:T(8,128)(2,1)} %get-tuple-element.67.refs_0_.refs_8_, ...), custom_call_target="tpu_custom_call" | custom-call | flops 34500001792 | tf_op jit(solution)/shard_map/forward_attention/pallas_call | solution.py:507
  151.6 141.9 %decoder_middle.1 = (bf16[384,768]{1,0:T(8,128)(2,1)}, bf16[384,768]{1,0:T(8,128)(2,1)}, bf16[384,768]{1,0:T(8,128)(2,1)}, f32[384,768]{1,0:T(8,128)}, f32[8,768...) custom-call(f32[1,384,768]{2,1,0:T(8,128)} %bitcast.72, ...), custom_call_target="tpu_custom_call" | custom-call | flops 92000002048 | tf_op jit(solution)/shard_map/decoder_middle/pallas_call | solution.py:507
  293.5 13.2 %projection_back.2 = (f32[8,768]{1,0:T(8,128)}, bf16[4,4,3,24,768]{4,3,2,1,0:T(8,128)(2,1)}, f32[384,18]{1,0:T(8,128)}, f32[18,768]{1,0:T(8,128)}) custom-call(bf16[384,768]{1,0:T(8,128)(2,1)} %get-tuple-element.80.refs_0_, bf16[384,768]{1,0:T(8,128)(2,1)} %get-tuple-element.81.refs_1_, bf16[384,768]{1,0:T(8,128)(2,1)} %get-tuple-element.82.refs_2_, ...), custom_call_target="tpu_custom_call" | custom-call | flops 13799999488 | tf_op jit(solution)/shard_map/projection_back/pallas_call | solution.py:507
  306.7 47.1 %forward_attention.3 = (bf16[1536,2304]{1,0:T(8,128)(2,1)}, bf16[384,768]{1,0:T(8,128)(2,1)}, bf16[384,768]{1,0:T(8,128)(2,1)}, f32[384,128]{1,0:T(8,128)}, bf16...) custom-call(bf16[4,384,768]{2,1,0:T(8,128)(2,1)} %get-tuple-element.78.refs_0_.refs_4_, ...), custom_call_target="tpu_custom_call" | custom-call | flops 34500001792 | tf_op jit(solution)/shard_map/forward_attention/pallas_call | solution.py:507
  353.8 140.3 %encoder_middle.1 = (bf16[384,768]{1,0:T(8,128)(2,1)}, bf16[384,768]{1,0:T(8,128)(2,1)}, bf16[384,768]{1,0:T(8,128)(2,1)}, f32[384,768]{1,0:T(8,128)}, f32[8,768...) custom-call(bf16[4,384,768]{2,1,0:T(8,128)(2,1)} %get-tuple-element., ...), custom_call_target="tpu_custom_call" | custom-call | flops 92000002048 | tf_op jit(solution)/shard_map/encoder_middle/pallas_call | solution.py:507
  494.1 50.6 %projection_back.3 = (f32[8,768]{1,0:T(8,128)}, bf16[4,4,3,24,768]{4,3,2,1,0:T(8,128)(2,1)}, f32[384,768]{1,0:T(8,128)}, f32[5,24,768]{2,1,0:T(8,128)}, f32[9,24,768]{2,1,0:T(8,128)}) custom-call(bf16[384,768]{1,0:T(8,128)(2,1)} %get-tuple-element.96.refs_0_, bf16[384,768]{1,0:T(8,128)(2,1)} %get-tuple-element.97.refs_1_, ...), custom_call_target="tpu_custom_call" | custom-call | flops 13799999488 | tf_op jit(solution)/shard_map/projection_back/pallas_call | solution.py:507
  544.7 0.9 slice.63
  545.6 0.9 slice.64
  546.5 1.2 fusion.5
  547.7 0.9 pad_maximum_fusion.1
  549.2 52.3 %last_sums.1 = (f32[3,24,768]{2,1,0:T(8,128)}, f32[64,768]{1,0:T(8,128)}) custom-call(bf16[4,4,3,24,768]{4,3,2,1,0:T(8,128)(2,1)} %get-tuple-element.104.refs_0_, f32[8,768]{1,0:T(8,128)} %get-tuple-element.105.refs_1_, f32[8,768]{1,0:T(8,128)} %get-tuple-element.106.refs_2_, f32[8,768]{1,0:T(8,128)} %get-tuple-element.107.refs_3_, ...), custom_call_target="tpu_custom_call" | custom-call | flops 34500001792 | tf_op jit(solution)/shard_map/last_sums/pallas_call | solution.py:507
  601.6 1.3 dynamic-slice_bitcast_fusion.1
  602.9 1.4 fusion.7
  604.3 1.4 fusion.8
  605.7 1.5 fusion.6
  607.2 0.8 slice.68
  608.7 0.7 copy.81
  609.4 1.1 copy.77
  611.2 0.9 pad_maximum_fusion
  612.3 0.8 pad_maximum_fusion.2
  613.1 0.8 copy.95
  614.0 1.0 copy.96
  (28 shorter events, 3.8 us)
Async XLA Ops:
  494.1 53.6 %copy-start.2 = (f32[4,24,768]{2,1,0:T(8,128)S(1)}, f32[4,24,768]{2,1,0:T(8,128)}, u32[]{:S(2)}) copy-start(f32[4,24,768]{2,1,0:T(8,128)} %get-tuple-element.118) | copy-start | bytes 884740
  607.2 4.9 copy-start.3
  610.7 2.4 copy-start.1
  611.0 2.9 copy-start

commit v2 on v1

--- a/solution.py
+++ b/solution.py
@@ -114,18 +114,19 @@
     def scratch(count):
         return [DMA((count, PARTS))] * 3
 
-    def __init__(self, here, arrays, sems):
-        self.here, self.arrays = here, arrays
+    def __init__(self, here, arrays, sems, sources=None):
+        self.here, self.arrays, self.sources = here, arrays, sources
         self.recv, self.up, self.down = sems
+
+    def at(self, m, block, z):
+        return self.arrays[m].at[relative(block, z) if self.sources is None else block]
 
     def copy(self, m, block, upward):
         z = self.here.z
         to = jnp.minimum(z + 1, PARTS - 1) if upward else jnp.maximum(z - 1, 0)
-        array = self.arrays[m]
         send = (self.up if upward else self.down).at[m, block]
-        return remote(
-            array.at[relative(block, z)], array.at[relative(block, to)], send, self.recv.at[m, block], (self.here.slot, to)
-        )
+        src = self.sources[m] if self.sources is not None and block is z else self.at(m, block, z)
+        return remote(src, self.at(m, block, to), send, self.recv.at[m, block], (self.here.slot, to))
 
     def onward(self, m, block, upward):
         z = self.here.z
@@ -291,6 +292,63 @@
         both.wait_recv()
 
 
+class Spread:
+    @staticmethod
+    def scratch(count):
+        return [DMA((11, count))]
+
+    def __init__(self, here, sources, outs, sems):
+        self.here, self.sources, self.outs, self.sems = here, sources, outs, sems[0]
+
+    def sem(self, m, n):
+        return self.sems.at[n, m]
+
+    def keep(self, m):
+        return pltpu.make_async_copy(self.sources[m], self.outs[m].at[self.here.slot], self.sem(m, 0))
+
+    def share(self, m, src, slot):
+        remote(src, self.outs[m].at[slot], self.sem(m, 1), self.sem(m, 2), self.here.sibling).start()
+
+    def side(self, m, n, src, slot):
+        peer = self.here.beside if n else self.here.across
+        return remote(src, self.outs[m].at[slot], self.sem(m, 3 + 2 * n), self.sem(m, 4 + 2 * n), peer)
+
+    def half(self, m, n, slot):
+        ref = self.outs[m].at[slot, pl.ds(n * (PARTS // 2), PARTS // 2)]
+        peer = self.here.across if n else self.here.beside
+        return remote(ref, ref, self.sem(m, 7 + 2 * n), self.sem(m, 8 + 2 * n), peer)
+
+    def start(self, m):
+        src, slot = self.sources[m], self.here.slot
+        for n in range(2):
+            self.side(m, n, src, slot).start()
+        self.keep(m).start()
+        self.share(m, src, slot)
+
+    def turn(self, m):
+        for n, peer in enumerate((self.here.across, self.here.beside)):
+            ref = self.outs[m].at[peer[0]]
+            self.side(m, n, ref, peer[0]).wait_recv()
+            self.half(m, n, peer[0]).start()
+            self.share(m, ref, peer[0])
+
+    def corner(self, m):
+        slot = flip(self.here.across[0], 2)
+        for n in range(2):
+            self.half(m, n, slot).wait_recv()
+        self.share(m, self.outs[m].at[slot], slot)
+
+    def finish(self, m):
+        self.keep(m).wait()
+        for n in range(2):
+            self.side(m, n, self.sources[m], self.here.slot).wait_send()
+            self.half(m, n, self.here.slot).wait_send()
+        four = self.outs[m].at[pl.ds(0, 4)]
+        both = remote(four, four, self.sem(m, 1), self.sem(m, 2), self.here.sibling)
+        both.wait_send()
+        both.wait_recv()
+
+
 def add_into(target, source):
     rows, units = target.shape[:2]
 
@@ -389,6 +447,59 @@
         lax.fori_loop(0, units, one, 0)
         for move in self.moves():
             move.wait_send()
+
+
+class Sum:
+    @staticmethod
+    def scratch(rows, width):
+        table, low = pltpu.VMEM((4, rows, width), F32), pltpu.VMEM((rows, width), BF16)
+        return [table, pltpu.VMEM((3, rows, width), F32), low, pltpu.VMEM((PARTS - 1, rows, width), BF16), DMA((2, 6))]
+
+    def __init__(self, here, sources, scratch):
+        self.here, self.sources = here, sources
+        self.tables, self.arrived, self.low, self.arrived_low, self.sems = scratch
+        self.peers = (here.sibling, here.across, here.beside)
+
+    def move(self, stage):
+        sems = self.sems
+        return remote(self.tables.at[stage], self.arrived.at[stage], sems.at[0, stage], sems.at[1, stage], self.peers[stage])
+
+    def stack(self, k):
+        sems = self.sems
+        return remote(self.low, self.arrived_low.at[k - 1], sems.at[0, 2 + k], sems.at[1, 2 + k], self.here.along(k))
+
+    def begin(self):
+        tables = self.tables
+        tables[0] = jnp.zeros_like(tables[0])
+        width = tables.shape[2]
+        at = 0
+        for source in self.sources:
+            rows, columns_held = source.shape
+            for start in range(0, columns_held, width):
+                tables[0, at : at + rows, :] = source[:, start : start + width]
+                at += rows
+        self.move(0).start()
+
+    def meet(self, stage):
+        self.move(stage).wait_recv()
+        self.tables[stage + 1] = self.tables[stage] + self.arrived[stage]
+        if stage < 2:
+            self.move(stage + 1).start()
+        else:
+            self.low[...] = self.tables[3].astype(BF16)
+            for k in range(1, PARTS):
+                self.stack(k).start()
+
+    def finish(self, out):
+        value = self.tables[3]
+        for k in range(1, PARTS):
+            self.stack(k).wait_recv()
+            value += self.arrived_low[k - 1].astype(F32)
+        out[...] = value
+        for stage in range(3):
+            self.move(stage).wait_send()
+        for k in range(1, PARTS):
+            self.stack(k).wait_send()
 
 
 class Cores:
@@ -545,7 +656,7 @@
     table[43:61, :] = ins["decode"][...].astype(F32)
     names = ("project", "output", "expand", "shrink")
     gather = Gather(
-        here, [table] + [ins[n].at[1] for n in names], [outs["table"]] + [outs[n] for n in names], own["gather"]
+        here, [table] + [ins[n].at[0] for n in names], [outs["table"]] + [outs[n] for n in names], own["gather"]
     )
     line = Line(here, [outs["signs"], outs["patches"]], own["line"])
     keeps = [
@@ -664,7 +775,8 @@
     return run(body, steps, ins, outs, scratch, collective, "forward_attention", 30)
 
 
-BLOCK = 128
+BLOCK = 192
+QUERY_BLOCK = 384
 
 
 def middle_block(encoder, layer, slots, ins, extra, collective):
@@ -681,23 +793,23 @@
     length = PARTS * rows
     first_query = feed + units
     first_key = first_query + pairs
-    steps = first_key + PARTS
+    steps = first_key + 2 * pairs
 
     def tiled(i):
         return lax.rem(jnp.minimum(i, feed - 1), tiles)
 
-    late = feed - tiles
+    tail = feed - tiles
     ins["expand"].spec = pl.BlockSpec((width, tile), lambda i: (0, tiled(i)))
     ins["expand_shift"].spec = pl.BlockSpec((1, tile), lambda i: (0, tiled(i)))
     ins["shrink"].spec = pl.BlockSpec((tile, width), lambda i: (tiled(i), 0))
     ins["stream"].spec = pl.BlockSpec((1, rows, width), lambda i: (0, 0, 0))
     outs = {
         "query": Item(shaped((rows, width)), pl.BlockSpec((rows, lanes), lambda i: (0, jnp.clip(i - first_query, 0, pairs - 1)))),
-        "key": Item(shaped((rows, width))),
-        "value": Item(shaped((rows, width))),
+        "key": Item(shaped((rows, width)), pl.BlockSpec((rows, lanes), lambda i: (0, jnp.maximum(i - first_key - pairs, 0)))),
+        "value": Item(shaped((rows, width)), pl.BlockSpec((rows, lanes), lambda i: (0, jnp.maximum(i - first_key - pairs, 0)))),
         "middle": Item(shaped((rows, width), F32)),
         "small": Item(shaped((8, width), F32)),
-        "wide": Item(shaped((1, hidden), F32), pl.BlockSpec((1, tile), lambda i: (0, jnp.clip(i - late, 0, tiles - 1)))),
+        "wide": Item(shaped((1, hidden), F32), pl.BlockSpec((1, tile), lambda i: (0, jnp.clip(i - tail, 0, tiles - 1)))),
     }
     scratch = {
         "active": pltpu.VMEM((rows, hidden), BF16),
@@ -725,7 +837,6 @@
         outs["decoded"] = Item(shaped((rows, width)))
         outs["sums"] = Item(shaped((4, PARTS, units, fine, width)))
     extra.declare(ins, outs, scratch)
-    extra.marks = {"feed": feed, "grads": feed, "query": first_query, "key": first_key}
 
     def body(here, step, ins, outs, own):
         table = ins["table"]
@@ -872,8 +983,8 @@
 
             keys, values = held[:, span(1)], held[:, span(2)]
             segments = ins["segment_row"][...]
-            for start in range(0, rows, BLOCK):
-                at = pl.ds(start, BLOCK)
+            for start in range(0, rows, QUERY_BLOCK):
+                at = pl.ds(start, QUERY_BLOCK)
                 same = ins["segment_column"][at, :] == segments
                 queries = held[at, span(0)] * eighth
                 grads = mixed_back[0, at, span(0)]
@@ -889,60 +1000,52 @@
                     parts.append(mm(score_low, keys) * HD**-0.5)
                 outs["query"][at, :] = jnp.where(lanes_of(0), parts[0], parts[1]).astype(BF16)
 
-        piece = step - first_key
-
-        @pl.when(piece == 2)
+        late = step - first_key
+
+        @pl.when(late == pairs)
         def _():
             for m in range(2):
                 line.hop(m, 3)
 
-        @pl.when(piece >= 0)
-        def _():
-            of_piece = pl.ds(pl.multiple_of(piece * rows, rows), rows)
-            segments = ins["segment_row"][:, of_piece]
-
-            def one(pair, carry):
+        for half in range(2):
+
+            @pl.when((late >= half * pairs) & (late < (half + 1) * pairs))
+            def _():
+                pair = late - half * pairs
+                pieces = range(2 * half, 2 * half + 2)
+
                 def span(part):
                     return pl.ds(pl.multiple_of(part * width + pair * lanes, lanes), lanes)
 
-                queries = held[of_piece, span(0)]
-                grads = mixed_back[piece, :, span(0)]
-                for start in range(0, rows, BLOCK):
-                    at = pl.ds(start, BLOCK)
-                    same = ins["segment_column"][at, :] == segments
-                    keys = held[at, span(1)] * eighth
-                    values = held[at, span(2)]
-                    key_parts, value_parts = [], []
-                    for head in range(2):
-                        log_sum = stats[piece, pl.ds(2 * pair + head, 1), :]
-                        centre = stats[piece, pl.ds(16 + 2 * pair + head, 1), :]
-                        scores = jnp.where(same, mm(only(keys, head), queries, NT), masked_score)
-                        probability = jnp.exp(scores - log_sum)
-                        value_parts.append(mm(probability.astype(BF16), grads))
-                        prob_grad = mm(only(values, head), grads, NT)
-                        score_low = (probability * (prob_grad - centre)).astype(BF16)
-                        key_parts.append(mm(score_low, queries) * HD**-0.5)
-                    key_part = jnp.where(lanes_of(0), key_parts[0], key_parts[1])
-                    value_part = jnp.where(lanes_of(0), value_parts[0], value_parts[1])
-
-                    @pl.when(piece == 0)
-                    def _():
-                        hat[at, span(0)] = key_part
-                        total[at, span(0)] = value_part
-
-                    @pl.when(piece > 0)
-                    def _():
-                        hat[at, span(0)] += key_part
-                        total[at, span(0)] += value_part
-
-                return carry
-
-            lax.fori_loop(0, pairs, one, 0)
-
-        @pl.when(piece == PARTS - 1)
-        def _():
-            outs["key"][...] = hat[...].astype(BF16)
-            outs["value"][...] = total[...].astype(BF16)
+                these = pl.ds(2 * half * rows, 2 * rows)
+                queries = held[these, span(0)]
+                grads = mixed_back[2 * half : 2 * half + 2, :, span(0)].reshape(2 * rows, lanes)
+
+                def line_of(row):
+                    return jnp.concatenate([stats[k, pl.ds(row, 1), :] for k in pieces], axis=1)
+
+                same = ins["segment_column"][...] == ins["segment_row"][:, these]
+                keys = held[pl.ds(0, rows), span(1)] * eighth
+                values = held[pl.ds(0, rows), span(2)]
+                key_parts, value_parts = [], []
+                for head in range(2):
+                    scores = jnp.where(same, mm(only(keys, head), queries, NT), masked_score)
+                    probability = jnp.exp(scores - line_of(2 * pair + head))
+                    value_parts.append(mm(probability.astype(BF16), grads))
+                    prob_grad = mm(only(values, head), grads, NT)
+                    score_low = (probability * (prob_grad - line_of(16 + 2 * pair + head))).astype(BF16)
+                    key_parts.append(mm(score_low, queries) * HD**-0.5)
+                key = jnp.where(lanes_of(0), key_parts[0], key_parts[1])
+                value = jnp.where(lanes_of(0), value_parts[0], value_parts[1])
+                if half == 0:
+                    hat[:, span(0)] = key
+                    total[:, span(0)] = value
+                else:
+                    outs["key"][...] = (hat[:, span(0)] + key).astype(BF16)
+                    outs["value"][...] = (total[:, span(0)] + value).astype(BF16)
+
+        @at_step(step, steps - 1)
+        def _():
             for m in range(2):
                 line.finish(m)
 
@@ -1009,57 +1112,18 @@
 def last_kernel(here, step, ins, outs, own):
     square = Square(here, own["square"][0], own["square"][1:], ins["sums"])
     stack = Stack(here, own["total"], own["stack"])
-    tables, arrived, sems = own["tables"], own["arrived"], own["sems"]
+    rows = Sum(here, [ins["small"]], own["sum"])
     square.load()
-    in0, in1, mid0, mid1 = (ins[n] for n in ("in0", "in1", "mid0", "mid1"))
-    rows = [in0[0:1], mid0[0:1], in1[0:1], mid1[0:1], in0[1:2], mid0[1:2], in1[1:2], mid1[1:2]]
-    rows += [in0[2:4], in1[2:4], mid0[2:3], mid1[2:3], mid0[3:4], mid1[3:4], in1[4:5]]
-    at = 0
-    tables[0] = jnp.zeros_like(tables[0])
-    for value in rows:
-        tables[0, at : at + value.shape[0], :] = value
-        at += value.shape[0]
-    width = tables.shape[2]
-    for wide in (ins["wide0"], ins["wide1"]):
-        for start in range(0, wide.shape[1], width):
-            tables[0, at : at + 1, :] = wide[:, start : start + width]
-            at += 1
-    for value in (ins["code_grad"], ins["decode_grad"]):
-        tables[0, at : at + value.shape[0], :] = value[...]
-        at += value.shape[0]
-
-    def move(stage, peer, k=0):
-        slot = stage + k
-        return remote(tables.at[stage], arrived.at[slot], sems.at[0, slot], sems.at[1, slot], peer)
-
-    peers = (here.sibling, here.across, here.beside)
-    move(0, peers[0]).start()
+    rows.begin()
     square.start()
-
-    def meet(stage):
-        move(stage, peers[stage]).wait_recv()
-        tables[stage + 1] = tables[stage] + arrived[stage]
-        if stage + 1 < len(peers):
-            move(stage + 1, peers[stage + 1]).start()
-
-    meet(0)
+    rows.meet(0)
+    rows.meet(1)
     square.sides()
-    meet(1)
+    rows.meet(2)
+    rows.finish(outs["rows"])
     square.total(own["total"])
     stack.start()
-    meet(2)
-    for k in range(1, PARTS):
-        move(3, here.along(k), k - 1).start()
     stack.finish(outs["units"])
-    value = tables[3]
-    for k in range(1, PARTS):
-        move(3, here.along(k), k - 1).wait_recv()
-        value += arrived[2 + k]
-    outs["table"][...] = value
-    for stage, peer in enumerate(peers):
-        move(stage, peer).wait_send()
-    for k in range(1, PARTS):
-        move(3, here.along(k), k - 1).wait_send()
 
 
 class Nothing:
@@ -1074,82 +1138,159 @@
 
 
 class Beside(Nothing):
-    def __init__(self, slots, gathers=None, gather_steps=(), squares=None, square_steps=None, stacks=None, stack_steps=None, inner=None):
+    def __init__(
+        self, slots, gathers=None, gather_steps=(), squares=None, stacks=None, sums=None, lines=None, line_steps=(), spreads=None, spread_steps=()
+    ):
+        self.lines, self.line_steps, self.spreads, self.spread_steps = lines or {}, line_steps, spreads or {}, spread_steps
         self.slots, self.gathers, self.gather_steps = slots, gathers or {}, gather_steps
-        self.squares, self.square_steps = squares or {}, square_steps or {}
-        self.stacks, self.stack_steps = stacks or {}, stack_steps or {}
-        self.inner = inner
+        self.squares, self.stacks, self.sums = squares or {}, stacks or {}, sums or {}
 
     def declare(self, ins, outs, scratch):
         for name, (array, layer) in self.gathers.items():
-            ins["shard_" + name] = anywhere(array)
+            block = (1,) + array.shape[1:]
+            ins["shard_" + name] = Item(array, pl.BlockSpec(block, lambda i, layer=layer: (layer, 0, 0)))
             outs["gathered_" + name] = anywhere(shaped((self.slots, PARTS) + array.shape[1:]))
         if self.gathers:
             scratch["gather"] = Gather.scratch(len(self.gathers))
-        for name, (sums, first, units) in self.squares.items():
-            ins["square_" + name] = anywhere(sums)
-            tail = sums.shape[3:]
+        for name, (array, layer) in self.lines.items():
+            block = (1,) + array.shape[1:]
+            ins["line_" + name] = Item(array, pl.BlockSpec(block, lambda i, layer=layer: (layer, 0, 0)))
+            outs["lined_" + name] = anywhere(shaped((PARTS,) + array.shape[1:]))
+        if self.lines:
+            scratch["lines"] = Line.scratch(len(self.lines)) + [DMA((len(self.lines),))]
+        for name, array in self.spreads.items():
+            ins["spread_" + name] = Item(array)
+            outs["gathered_" + name] = anywhere(shaped((self.slots,) + array.shape))
+        if self.spreads:
+            scratch["spreads"] = Spread.scratch(len(self.spreads))
+        for name, (sums, first, units, steps) in self.squares.items():
+            loaded = sums is not None
+            if loaded:
+                tail = sums.shape[3:]
+            else:
+                tail = (scratch["sums"] if "sums" in scratch else outs["sums"].array).shape[3:]
+            if loaded:
+                ins["square_" + name] = anywhere(sums)
             outs["total_" + name] = Item(shaped((PARTS, units) + tail))
-            scratch["square_" + name] = Square.scratch(units, tail, True)
-        for name, array in self.stacks.items():
-            ins["stack_" + name] = Item(array)
-            outs["stacked_" + name] = Item(shaped(array.shape[1:], F32))
-            scratch["stack_" + name] = Stack.scratch(array.shape[1], array.shape[2:])
-        if self.inner:
-            name, units = self.inner
-            shape = scratch["sums"].shape
-            outs["total_" + name] = Item(shaped(shape[1:]))
-            scratch["inner"] = Square.scratch(units, shape[3:], False)
-
-    def events(self, here, step, steps, ins, outs, own):
+            scratch["square_" + name] = Square.scratch(units, tail, loaded)
+        for name, (array, steps) in self.stacks.items():
+            if isinstance(array, str):
+                shape = outs["total_" + array].array.shape
+            else:
+                ins["stack_" + name] = Item(array)
+                shape = array.shape
+            outs["stacked_" + name] = Item(shaped(shape[1:], F32))
+            scratch["stack_" + name] = Stack.scratch(shape[1], shape[2:])
+        for name, (arrays, steps) in self.sums.items():
+            for i, array in enumerate(arrays):
+                ins[f"sum_{name}{i}"] = Item(array)
+            width = min(a.shape[1] for a in arrays)
+            rows = -(-sum(a.shape[0] * (a.shape[1] // width) for a in arrays) // 16) * 16
+            outs["summed_" + name] = Item(shaped((rows, width), F32))
+            scratch["sum_" + name] = Sum.scratch(rows, width)
+
+    def listed(self, here, ins, outs, own):
         if self.gathers:
             names = list(self.gathers)
-            sources = [ins["shard_" + n].at[self.gathers[n][1]] for n in names]
-            gather = Gather(here, sources, [outs["gathered_" + n] for n in names], own["gather"])
-            count = range(len(names))
+            gather = Gather(here, [ins["shard_" + n].at[0] for n in names], [outs["gathered_" + n] for n in names], own["gather"])
 
             def each(*actions):
-                for action, *more in actions:
-                    for m in count:
-                        action(m, *more)
+                def go():
+                    for action, *more in actions:
+                        for m in range(len(names)):
+                            action(m, *more)
+
+                return go
 
             start, one, two, three, turn, corner = self.gather_steps
-            stages = [
-                (start, [(gather.start,)]),
-                (one, [(gather.hop, 1), (gather.turn, 0)]),
-                (two, [(gather.hop, 2), (gather.turn, 1)]),
-                (three, [(gather.hop, 3), (gather.turn, 2)]),
-                (turn, [(gather.turn, 3), (gather.siblings,)]),
-                (corner, [(gather.corner,)]),
-                (steps - 1, [(gather.finish,)]),
-            ]
-            for n, actions in stages:
-                at_step(step, n)(lambda actions=actions: each(*actions))
-        for name, (sums, first, units) in self.squares.items():
+            yield start, each((gather.start,))
+            yield one, each((gather.hop, 1), (gather.turn, 0))
+            yield two, each((gather.hop, 2), (gather.turn, 1))
+            yield three, each((gather.hop, 3), (gather.turn, 2))
+            yield turn, each((gather.turn, 3), (gather.siblings,))
+            yield corner, each((gather.corner,))
+            yield None, each((gather.finish,))
+        if self.lines:
+            line_names = list(self.lines)
+            sources = [ins["line_" + n].at[0] for n in line_names]
+            arrays = [outs["lined_" + n] for n in line_names]
+            sems = own["lines"]
+            line = Line(here, arrays, sems[:3], sources)
+            keeps = [pltpu.make_async_copy(sources[m], arrays[m].at[here.z], sems[3].at[m]) for m in range(len(line_names))]
+
+            def begin():
+                for m in range(len(line_names)):
+                    line.start(m)
+                    keeps[m].start()
+
+            def end():
+                for m in range(len(line_names)):
+                    line.finish(m)
+                    keeps[m].wait()
+
+            def hop(k):
+                for m in range(len(line_names)):
+                    line.hop(m, k)
+
+            yield self.line_steps[0], begin
+            for k in range(1, PARTS):
+                yield self.line_steps[k], functools.partial(hop, k)
+            yield None, end
+        if self.spreads:
+            spread_names = list(self.spreads)
+            spread = Spread(here, [ins["spread_" + n] for n in spread_names], [outs["gathered_" + n] for n in spread_names], own["spreads"])
+            for action, n in zip((spread.start, spread.turn, spread.corner, spread.finish), self.spread_steps):
+
+                def go(action=action):
+                    for m in range(len(spread_names)):
+                        action(m)
+
+                yield n, go
+        for name, (sums, first, units, steps) in self.squares.items():
             scratch = own["square_" + name]
-            square = Square(here, scratch[0], scratch[1:], ins["square_" + name].at[:, :, pl.ds(first, units)])
-            load, start, sides, total = self.square_steps[name]
-            at_step(step, load)(square.load)
-            at_step(step, start)(square.start)
-            at_step(step, sides)(square.sides)
-            at_step(step, total)(lambda square=square, name=name: square.total(outs["total_" + name]))
-        for name in self.stacks:
-            stack = Stack(here, ins["stack_" + name], own["stack_" + name])
-            start, finish = self.stack_steps[name]
-            at_step(step, start)(stack.start)
-            at_step(step, finish)(lambda stack=stack, name=name: stack.finish(outs["stacked_" + name]))
-        if self.inner:
-            name, units = self.inner
-            square = Square(here, own["sums"], own["inner"])
-            start, sides = self.square_steps[name]
-            at_step(step, start)(square.start)
-            at_step(step, sides)(square.sides)
+            span = pl.ds(first, units)
+            if sums is None:
+                held = own["sums"] if "sums" in own else outs["sums"]
+                square = Square(here, held.at[:, :, span], scratch)
+            else:
+                square = Square(here, scratch[0], scratch[1:], ins["square_" + name].at[:, :, span])
+                yield steps[0], square.load
+            yield steps[1], square.start
+            yield steps[2], square.sides
+            yield steps[3], functools.partial(square.total, outs["total_" + name])
+        for name, (array, steps) in self.stacks.items():
+            held = outs["total_" + array] if isinstance(array, str) else ins["stack_" + name]
+            stack = Stack(here, held, own["stack_" + name])
+            yield steps[0], stack.start
+            yield steps[1], functools.partial(stack.finish, outs["stacked_" + name])
+        for name, (arrays, steps) in self.sums.items():
+            rows = Sum(here, [ins[f"sum_{name}{i}"] for i in range(len(arrays))], own["sum_" + name])
+            yield steps[0], rows.begin
+            for stage in range(3):
+                yield steps[1 + stage], functools.partial(rows.meet, stage)
+            yield steps[4], functools.partial(rows.finish, outs["summed_" + name])
+
+    def grouped(self, here, ins, outs, own):
+        groups = {}
+        for n, action in self.listed(here, ins, outs, own):
+            groups.setdefault(n, []).append(action)
+        return groups
+
+    def play(self, step, n, actions):
+        def go():
+            for action in actions:
+                action()
+
+        at_step(step, n)(go)
+
+    def events(self, here, step, steps, ins, outs, own):
+        for n, actions in sorted((n, a) for n, a in self.grouped(here, ins, outs, own).items() if n is not None):
+            self.play(step, n, actions)
 
     def closing(self, here, step, steps, ins, outs, own):
-        if self.inner:
-            name, units = self.inner
-            square = Square(here, own["sums"], own["inner"])
-            at_step(step, steps - 1)(lambda: square.total(outs["total_" + name]))
+        actions = self.grouped(here, ins, outs, own).get(None)
+        if actions:
+            self.play(step, steps - 1, actions)
 
 
 def on_device(
@@ -1209,8 +1350,9 @@
         "decode": Item(decode_weight),
     }
     weights = {"project": project_weight, "output": output_weight, "expand": expand_weight, "shrink": shrink_weight}
-    for name, array in (("signs", signs), ("patches", patches), *weights.items()):
-        ins[name] = anywhere(array)
+    ins["signs"], ins["patches"] = Item(signs), Item(patches)
+    for name, array in weights.items():
+        ins[name] = Item(array, pl.BlockSpec((1,) + array.shape[1:], lambda i: (1, 0, 0)))
     outs = {
         "table": anywhere(shaped((slots, parts, 64, fine), F32)),
         "signs": anywhere(shaped((parts, rows, CODE))),
@@ -1279,66 +1421,78 @@
         return projection_back(layer == 1, layer, slots, ins, extra, collective)
 
     decoder = {n: flat(first[n]) for n in weights}
-    beside = Beside(slots, {n: (weights[n], 0) for n in ("project", "output")}, (0, 2, 4, 5, 7, 8))
+    names = ("output", "expand", "shrink")
+    beside = Beside(
+        slots,
+        {"project": (project_weight, 0)},
+        (0, 2, 4, 5, 7, 9),
+        lines={n: (weights[n], 0) for n in names},
+        line_steps=(1, 4, 7, None),
+    )
     ahead1 = forward(1, first["signs"], decoder["project"], beside, 1)
-    encoder = {n: flat(ahead1["gathered_" + n]) for n in ("project", "output")}
-
-    beside = Beside(slots, {n: (weights[n], 0) for n in ("expand", "shrink")}, (0, 3, 6, 9, 14, 18))
+    encoder = {"project": flat(ahead1["gathered_project"])}
+
+    beside = Beside(
+        slots,
+        spreads={n: ahead1["lined_" + n] for n in names},
+        spread_steps=(0, 12, 18, None),
+        squares={"two": (None, 0, 4, (None, 13, 20, 27))},
+    )
     stream1 = ahead1["stream"][None]
     between1 = middle(1, stream1, cotangent[0], ahead1, decoder, beside, 2)
-    encoder.update({n: flat(between1["gathered_" + n]) for n in ("expand", "shrink")})
-    after1 = projection(1, stream1, ahead1, between1, decoder["project"], Nothing(), 3, pieces=first["signs"])
+    encoder.update({n: flat(between1["gathered_" + n]) for n in names})
+    beside = Beside(slots, stacks={"two": (between1["total_two"], (0, 3))})
+    after1 = projection(1, stream1, ahead1, between1, decoder["project"], beside, 3, pieces=first["signs"])
 
     beside = Beside(
         slots,
-        squares={"one": (after1["sums"], 0, 3), "two": (between1["sums"], 0, 4)},
-        square_steps={"one": (0, 1, 3, 6), "two": (0, 1, 4, 9)},
+        squares={"three": (between1["sums"], 4, 5, (0, 1, 5, None))},
+        sums={"one": ([after1["small"], between1["small"], between1["wide"], after1["decode_grad"]], (0, 1, 3, 5, None))},
     )
     ahead0 = forward(0, first["patches"], encoder["project"], beside, 4)
     beside = Beside(
         slots,
-        squares={"three": (between1["sums"], 4, 5)},
-        square_steps={"three": (0, 1, 5, 12), "inner": (22, 26)},
-        stacks={n: ahead0["total_" + n] for n in ("one", "two")},
-        stack_steps={"one": (0, 8), "two": (2, 10)},
-        inner=("inner", 9),
+        squares={
+            "one": (after1["sums"], 0, 3, (0, 1, 4, 9)),
+            "five": (None, 0, 4, (None, 18, 22, 28)),
+            "six": (None, 4, 5, (None, 22, 30, None)),
+        },
+        stacks={
+            "three": (ahead0["total_three"], (0, 9)),
+            "one": ("one", (10, 18)),
+            "five": ("five", (33, None)),
+        },
     )
     between0 = middle(0, first["patches"], after1["unit_grad"], ahead0, encoder, beside, 5)
     beside = Beside(
         slots,
-        stacks={"three": between0["total_three"], "inner": between0["total_inner"]},
-        stack_steps={"three": (0, 3), "inner": (0, 3)},
+        stacks={"six": (between0["total_six"], (0, 3))},
+        sums={"two": ([between0["small"], between0["wide"], between0["code_grad"]], (0, 1, 2, 3, None))},
     )
     after0 = projection(0, first["patches"], ahead0, between0, encoder["project"], beside, 6)
 
-    ins = {
-        "sums": anywhere(after0["sums"]),
-        "in0": Item(after0["small"]),
-        "in1": Item(after1["small"]),
-        "mid0": Item(between0["small"]),
-        "mid1": Item(between1["small"]),
-        "wide0": Item(between0["wide"]),
-        "wide1": Item(between1["wide"]),
-        "code_grad": Item(between0["code_grad"]),
-        "decode_grad": Item(after1["decode_grad"]),
-    }
-    outs = {"units": Item(shaped((3, fine, width), F32)), "table": Item(shaped((64, width), F32))}
+    ins = {"sums": anywhere(after0["sums"]), "small": Item(after0["small"])}
+    outs = {"units": Item(shaped((3, fine, width), F32)), "rows": Item(shaped((16, width), F32))}
     scratch = {
         "square": Square.scratch(3, (fine, width), True),
         "total": pltpu.VMEM((parts, 3, fine, width), BF16),
         "stack": Stack.scratch(3, (fine, width)),
-        "tables": pltpu.VMEM((4, 64, width), F32),
-        "arrived": pltpu.VMEM((6, 64, width), F32),
-        "sems": DMA((2, 6)),
+        "sum": Sum.scratch(16, width),
     }
     last = run(last_kernel, 1, ins, outs, scratch, 7, "last_sums", 30)
 
     device = slot * parts + z
-    mine = lax.dynamic_slice(last["table"], (0, device * fine), (64, fine))
-    wide = last["table"][17:25].reshape(2, hidden)
+    one, two = ahead0["summed_one"], after0["summed_two"]
+    summed = jnp.concatenate([last["rows"][:8], one, two])
+    mine = lax.dynamic_slice(summed, (0, device * fine), (summed.shape[0], fine))
+    in0, in1, mid1 = mine[0:4], mine[8:13], mine[16:20]
+    at = 8 + one.shape[0]
+    mid0, decode_grad, code_grad = mine[at : at + 4], mine[28:46], mine[at + 12 : at + 30]
+    wide = jnp.stack([two[8:12].reshape(hidden), one[16:20].reshape(hidden)])
     wide = lax.dynamic_slice(wide, (0, device * (hidden // devices)), (2, hidden // devices))
-    decoder_mlp = jnp.concatenate([between0["stacked_two"], after0["stacked_three"]])
-    encoder_mlp, encoder_project, decoder_project = after0["stacked_inner"], last["units"], between0["stacked_one"]
+    decoder_mlp = jnp.concatenate([after1["stacked_two"], between0["stacked_three"]])
+    encoder_mlp = jnp.concatenate([between0["stacked_five"], after0["stacked_six"]])
+    encoder_project, decoder_project = last["units"], between0["stacked_one"]
 
     def both(cut):
         return jnp.stack([cut(encoder_mlp), cut(decoder_mlp)])
@@ -1349,19 +1503,19 @@
     return (
         between1["decoded"][None],
         after0["grad"][None],
-        mine[0:4].reshape(2, 2, fine),
-        mine[4:8].reshape(2, 2, fine),
+        jnp.stack([jnp.stack([in0[0], mid0[0]]), jnp.stack([in1[0], mid1[0]])]),
+        jnp.stack([jnp.stack([in0[1], mid0[1]]), jnp.stack([in1[1], mid1[1]])]),
         jnp.stack([joined(encoder_project), joined(decoder_project)]),
-        mine[8:12].reshape(2, 2, fine),
+        jnp.stack([in0[2:4], in1[2:4]]),
         both(lambda g: g[8]),
-        mine[12:14],
+        jnp.stack([mid0[2], mid1[2]]),
         both(lambda g: joined(g[4:8])),
         wide,
         both(lambda g: g[0:4].reshape(4 * fine, width)),
-        mine[14:16],
-        mine[25:43].T,
-        mine[43:61],
-        mine[16],
+        jnp.stack([mid0[3], mid1[3]]),
+        code_grad.T,
+        decode_grad,
+        in1[4],
     )
 
 

time: 624 us -> 483 us (0.77)
  Pallas kernels: 587 us -> 450 us
    pallas_call x8, Pallas kernels: 587 us -> 450 us  [run(): pl.pallas_call(kernel, grid=(steps,), in_specs=[i.spec for i in ins.value...]
where the time goes in v2:
time: 483 us; the launch traced here: 476 us
  Pallas kernels  450 us (93%)
  local copies, waits for them, and re-layouts  17 us (4%)
  other arithmetic  7.75 us (2%)
    pallas_call x8, Pallas kernels, run(): pl.pallas_call(kernel, grid=(steps,), in_specs=[i.spec for i in ins.value...  450 us

profile of v2, /device:TPU:0, one launch (start us, length us, event | category | flops | bytes accessed | tf_op | source)
XLA Modules:
  0.0 476.1 jit_solution(10561080629310475305)
XLA Ops:
  0.7 0.7 reduce
  2.0 0.6 copy.83
  2.6 0.8 fusion.5
  3.3 0.8 copy.62.refs_9_
  4.1 0.8 copy.65.refs_4_.refs_11_
  4.9 89.3 %first_gather.1 = (f32[8,4,64,24]{3,2,1,0:T(8,128)}, bf16[4,384,18]{2,1,0:T(8,128)(2,1)}, bf16[4,384,768]{2,1,0:T(8,128)(2,1)}, bf16[8,4,24,2304]{3,2,1,0:T(8,12...) custom-call(bf16[2,2,24]{2,1,0:T(2,128)(2,1)} %refs_0_.1, ...), custom_call_target="tpu_custom_call" | custom-call | flops 80499998720 | tf_op jit(solution)/shard_map/first_gather/pallas_call | solution.py:618
  94.2 1.0 slice.136
  95.2 1.5 copy.63
  96.9 0.8 copy.64.refs_1_.refs_5_.refs_6_
  97.8 0.7 squeeze.14.refs_8_
  98.6 0.7 squeeze.13.refs_8_
  99.4 40.0 %forward_attention.2 = (bf16[1536,2304]{1,0:T(8,128)(2,1)}, bf16[384,768]{1,0:T(8,128)(2,1)}, bf16[384,768]{1,0:T(8,128)(2,1)}, f32[384,128]{1,0:T(8,128)}, f32[...) custom-call(bf16[4,384,18]{2,1,0:T(8,128)(2,1)} %get-tuple-element.7, ...), custom_call_target="tpu_custom_call" | custom-call | flops 34500001792 | tf_op jit(solution)/shard_map/forward_attention/pallas_call | solution.py:618
  139.3 94.0 %decoder_middle.1 = (bf16[384,768]{1,0:T(8,128)(2,1)}, bf16[384,768]{1,0:T(8,128)(2,1)}, bf16[384,768]{1,0:T(8,128)(2,1)}, f32[384,768]{1,0:T(8,128)}, f32[8,768...) custom-call(f32[1,384,768]{2,1,0:T(8,128)} %bitcast.88, ...), custom_call_target="tpu_custom_call" | custom-call | flops 92000002048 | tf_op jit(solution)/shard_map/decoder_middle/pallas_call | solution.py:618
  233.3 21.5 %projection_back.2 = (f32[8,768]{1,0:T(8,128)}, bf16[4,4,3,24,768]{4,3,2,1,0:T(8,128)(2,1)}, f32[384,18]{1,0:T(8,128)}, f32[18,768]{1,0:T(8,128)}, f32[4,24,768]{2,1,0:T(8,128)}) custom-call(bf16[384,768]{1,0:T(8,128)(2,1)} %get-tuple-element.89.refs_0_, bf16[384,768]{1,0:T(8,128)(2,1)} %get-tuple-element.90.refs_1_, ...), custom_call_target="tpu_custom_call" | custom-call | flops 13799999488 | tf_op jit(solution)/shard_map/projection_back/pallas_call | solution.py:618
  254.8 41.9 %forward_attention.3 = (bf16[1536,2304]{1,0:T(8,128)(2,1)}, bf16[384,768]{1,0:T(8,128)(2,1)}, bf16[384,768]{1,0:T(8,128)(2,1)}, f32[384,128]{1,0:T(8,128)}, bf16...) custom-call(bf16[4,384,768]{2,1,0:T(8,128)(2,1)} %get-tuple-element.86.refs_0_.refs_4_, ...), custom_call_target="tpu_custom_call" | custom-call | flops 34500001792 | tf_op jit(solution)/shard_map/forward_attention/pallas_call | solution.py:618
  296.8 101.7 %encoder_middle.1 = (bf16[384,768]{1,0:T(8,128)(2,1)}, bf16[384,768]{1,0:T(8,128)(2,1)}, bf16[384,768]{1,0:T(8,128)(2,1)}, f32[384,768]{1,0:T(8,128)}, f32[8,768...) custom-call(bf16[4,384,768]{2,1,0:T(8,128)(2,1)} %get-tuple-element., ...), custom_call_target="tpu_custom_call" | custom-call | flops 92000002048 | tf_op jit(solution)/shard_map/encoder_middle/pallas_call | solution.py:618
  398.5 29.6 %projection_back.3 = (f32[8,768]{1,0:T(8,128)}, bf16[4,4,3,24,768]{4,3,2,1,0:T(8,128)(2,1)}, f32[384,768]{1,0:T(8,128)}, f32[5,24,768]{2,1,0:T(8,128)}, f32[32,768]{1,0:T(8,128)}) custom-call(bf16[384,768]{1,0:T(8,128)(2,1)} %get-tuple-element.108.refs_0_, bf16[384,768]{1,0:T(8,128)(2,1)} %get-tuple-element.109.refs_1_, ...), custom_call_target="tpu_custom_call" | custom-call | flops 13799999488 | tf_op jit(solution)/shard_map/projection_back/pallas_call | solution.py:618
  428.1 0.7 slice_bitcast_fusion.4
  428.9 0.6 fusion.6
  429.5 0.9 slice.120
  430.4 1.0 slice_bitcast_fusion.1
  432.0 0.9 pad_maximum_fusion
  432.9 0.7 pad_maximum_fusion.3
  433.5 32.1 %last_sums.1 = (f32[3,24,768]{2,1,0:T(8,128)}, f32[16,768]{1,0:T(8,128)}) custom-call(bf16[4,4,3,24,768]{4,3,2,1,0:T(8,128)(2,1)} %get-tuple-element.118.refs_0_, f32[8,768]{1,0:T(8,128)} %get-tuple-element.119.refs_1_), custom_call_target="tpu_custom_call" | custom-call | flops 34500001792 | tf_op jit(solution)/shard_map/last_sums/pallas_call | solution.py:618
  465.7 0.8 slice.109
  467.8 0.6 fusion.9
  470.1 0.7 copy.81
  470.8 1.1 copy.77
  472.3 0.8 pad_maximum_fusion.2
  473.1 0.9 pad_maximum_fusion.1
  474.0 0.8 copy.97
  474.8 1.0 copy.98
  (46 shorter events, 4.9 us)
Async XLA Ops:
  398.5 30.3 %copy-start.6 = (f32[48,768]{1,0:T(8,128)S(1)}, f32[48,768]{1,0:T(8,128)}, u32[]{:S(2)}) copy-start(f32[48,768]{1,0:T(8,128)} %get-tuple-element.121) | copy-start | bytes 442372
  398.5 33.2 %copy-start.2 = (f32[5,24,768]{2,1,0:T(8,128)S(1)}, f32[5,24,768]{2,1,0:T(8,128)}, u32[]{:S(2)}) copy-start(f32[5,24,768]{2,1,0:T(8,128)} %get-tuple-element.126) | copy-start | bytes 1105924
  433.5 33.0 %copy-start.7 = (f32[32,768]{1,0:T(8,128)S(1)}, f32[32,768]{1,0:T(8,128)}, u32[]{:S(2)}) copy-start(f32[32,768]{1,0:T(8,128)} %get-tuple-element.122) | copy-start | bytes 294916
  433.5 38.5 %copy-start.5 = (f32[3,24,768]{2,1,0:T(8,128)S(1)}, f32[3,24,768]{2,1,0:T(8,128)}, u32[]{:S(2)}) copy-start(f32[3,24,768]{2,1,0:T(8,128)} %get-tuple-element.124) | copy-start | bytes 663556
  465.7 7.4 %copy-start.3 = (f32[4,24,768]{2,1,0:T(8,128)S(1)}, f32[4,24,768]{2,1,0:T(8,128)}, u32[]{:S(2)}) copy-start(f32[4,24,768]{2,1,0:T(8,128)} %get-tuple-element.128) | copy-start | bytes 884740
  465.7 7.4 %copy-start.4 = (f32[4,24,768]{2,1,0:T(8,128)S(1)}, f32[4,24,768]{2,1,0:T(8,128)}, u32[]{:S(2)}) copy-start(f32[4,24,768]{2,1,0:T(8,128)} %get-tuple-element.127) | copy-start | bytes 884740
  465.7 8.3 %copy-start.1 = (bf16[384,768]{1,0:T(8,128)(2,1)S(1)}, bf16[384,768]{1,0:T(8,128)(2,1)}, u32[]{:S(2)}) copy-start(bf16[384,768]{1,0:T(8,128)(2,1)} %get-tuple-element.85) | copy-start | bytes 1769476
  471.9 3.0 copy-start

commit v3 on v2

--- a/solution.py
+++ b/solution.py
@@ -114,12 +114,12 @@
     def scratch(count):
         return [DMA((count, PARTS))] * 3
 
-    def __init__(self, here, arrays, sems, sources=None):
-        self.here, self.arrays, self.sources = here, arrays, sources
+    def __init__(self, here, arrays, sems, sources, absolute):
+        self.here, self.arrays, self.sources, self.absolute = here, arrays, sources, absolute
         self.recv, self.up, self.down = sems
 
     def at(self, m, block, z):
-        return self.arrays[m].at[relative(block, z) if self.sources is None else block]
+        return self.arrays[m].at[block if self.absolute[m] else relative(block, z)]
 
     def copy(self, m, block, upward):
         z = self.here.z
@@ -163,6 +163,41 @@
             @pl.when((z > 0) & (z <= block))
             def _():
                 self.copy(m, block, False).wait_send()
+
+
+class Hop:
+    @staticmethod
+    def scratch():
+        return [DMA((4,))]
+
+    def __init__(self, here, k, source, out, sems):
+        self.here, self.k, self.source, self.out, self.sems = here, k, source, out, sems[0]
+
+    def copy(self, upward, block):
+        z = self.here.z
+        to = jnp.minimum(z + 1, PARTS - 1) if upward else jnp.maximum(z - 1, 0)
+        src = self.source if self.k == 1 else self.source.at[relative(block, z)]
+        n = 0 if upward else 2
+        return remote(src, self.out.at[relative(block, to)], self.sems.at[n], self.sems.at[n + 1], (self.here.slot, to))
+
+    def start(self, wait=False):
+        z, back = self.here.z, self.k - 1
+        for upward, meets in ((True, (z >= back) & (z < PARTS - 1)), (False, (z + back <= PARTS - 1) & (z > 0))):
+
+            @pl.when(meets)
+            def _():
+                move = self.copy(upward, z - back if upward else z + back)
+                move.wait_send() if wait else move.start()
+
+    def finish(self):
+        z, k = self.here.z, self.k
+        for upward, meets in ((True, z >= k), (False, z + k <= PARTS - 1)):
+
+            @pl.when(meets)
+            def _():
+                self.copy(upward, jnp.clip(z, 0, PARTS - 1)).wait_recv()
+
+        self.start(True)
 
 
 class Gather:
@@ -350,14 +385,11 @@
 
 
 def add_into(target, source):
-    rows, units = target.shape[:2]
-
-    def one(i, carry):
-        a, b = i // units, lax.rem(i, units)
-        target[a, b] = (target[a, b].astype(F32) + source[a, b].astype(F32)).astype(target.dtype)
+    def one(a, carry):
+        target[a] = (target[a].astype(F32) + source[a].astype(F32)).astype(target.dtype)
         return carry
 
-    lax.fori_loop(0, rows * units, one, 0)
+    lax.fori_loop(0, target.shape[0], one, 0)
 
 
 class Square:
@@ -401,15 +433,13 @@
     def total(self, out):
         self.move(2).wait_recv()
         self.move(3).wait_recv()
-        units = out.shape[1]
-
-        def one(i, carry):
-            a, b = i // units, lax.rem(i, units)
-            value = self.held[0, a, b].astype(F32) + self.side_x[a, b].astype(F32) + self.side_y[a, b].astype(F32)
-            out[a, b] = value.astype(out.dtype)
+
+        def one(a, carry):
+            value = self.held[0, a].astype(F32) + self.side_x[a].astype(F32) + self.side_y[a].astype(F32)
+            out[a] = value.astype(out.dtype)
             return carry
 
-        lax.fori_loop(0, PARTS * units, one, 0)
+        lax.fori_loop(0, PARTS, one, 0)
         for n in range(4):
             self.move(n).wait_send()
 
@@ -565,14 +595,13 @@
                 at = relative(self.here.square, n)
                 add_into(self.sums.at[at, :, pl.ds(0, self.hidden)], self.far.at[at, :, pl.ds(0, self.hidden)])
             else:
-                for s in range(4):
-
-                    def one(a, carry):
-                        value = self.sums[s, a, n].astype(F32) + self.far[s, a, n].astype(F32)
-                        self.sums[s, a, n] = value.astype(BF16)
-                        return carry
-
-                    lax.fori_loop(0, PARTS, one, 0)
+
+                def one(s, carry):
+                    value = self.sums[s, :, n].astype(F32) + self.far[s, :, n].astype(F32)
+                    self.sums[s, :, n] = value.astype(BF16)
+                    return carry
+
+                lax.fori_loop(0, 4, one, 0)
 
         self.each(n, action)
 
@@ -654,47 +683,37 @@
         table[17 + i : 18 + i, :] = wide[i // 4 : i // 4 + 1, fine * (i % 4) : fine * (i % 4 + 1)]
     table[25:43, :] = ins["encode"][...].astype(F32).T
     table[43:61, :] = ins["decode"][...].astype(F32)
-    names = ("project", "output", "expand", "shrink")
-    gather = Gather(
-        here, [table] + [ins[n].at[0] for n in names], [outs["table"]] + [outs[n] for n in names], own["gather"]
-    )
-    line = Line(here, [outs["signs"], outs["patches"]], own["line"])
-    keeps = [
-        pltpu.make_async_copy(ins[n].at[0], outs[n].at[0], own["keep"].at[i]) for i, n in enumerate(("signs", "patches"))
-    ]
-    messages = range(len(names) + 1)
-    gather.start(0)
-    for keep in keeps:
-        keep.start()
-    for m in messages[1:]:
+    gather = Gather(here, [table, ins["project"].at[0]], [outs["table"], outs["project"]], own["gather"])
+    signs = ins["signs"].at[0]
+    line = Line(here, [outs["signs"]], own["line"], [signs], (False,))
+    keep = pltpu.make_async_copy(signs, outs["signs"].at[0], own["keep"].at[0])
+    patches = Hop(here, 1, ins["patches"].at[0], outs["patches"], own["patches"])
+    for m in range(2):
         gather.start(m)
-    for keep in keeps:
-        keep.wait()
     line.start(0)
+    keep.start()
+    patches.start()
     for k in range(1, PARTS):
+        for m in range(2):
+            gather.hop(m, k)
         line.hop(0, k)
-        for m in messages:
-            gather.hop(m, k)
+        for m in range(2):
             gather.turn(m, k - 1)
-        if k == 1:
-            line.start(1)
-        else:
-            line.hop(1, k - 1)
-    for m in messages:
+    for m in range(2):
         gather.turn(m, PARTS - 1)
         gather.siblings(m)
-    line.hop(1, PARTS - 1)
-    for m in messages:
+    for m in range(2):
         gather.corner(m)
-    for m in messages:
+    for m in range(2):
         gather.finish(m)
-    for m in range(2):
-        line.finish(m)
+    line.finish(0)
+    patches.finish()
+    keep.wait()
 
 
 def forward_attention(coded, layer, slots, ins, extra, collective):
-    pieces, table, weight = ins["pieces"].array, ins["table"].array, ins["weight"].array
-    rows = pieces.shape[1]
+    weight = ins["weight"].array
+    rows = ins["segment_column"].array.shape[0]
     width, triple = weight.shape
     length = PARTS * rows
     pairs, lanes = width // (2 * HD), 2 * HD
@@ -707,7 +726,7 @@
     }
     if coded:
         outs["stream"] = Item(shaped((rows, width), F32))
-    scratch = {"qkv_held": pltpu.VMEM((length, triple), BF16)}
+    scratch = {"qkv_held": pltpu.VMEM((length, triple), BF16), "piece": pltpu.VMEM((rows, width), BF16)}
     extra.declare(ins, outs, scratch)
 
     def body(here, step, ins, outs, own):
@@ -721,7 +740,15 @@
                 decode = table[43:61, :].astype(BF16)
                 stream = mm(ins["pieces"][step], decode) + table[16:17, :]
             else:
-                stream = ins["pieces"][step].astype(F32)
+                inner = (here.z > 0) & (here.z < PARTS - 1)
+                choices = [step == 0, step == 1, step == 2, (step == 3) & inner, (step == 3) & jnp.logical_not(inner)]
+                for n, meets in enumerate(choices):
+
+                    @pl.when(meets)
+                    def _():
+                        own["piece"][...] = ins[f"piece{n}"][0]
+
+                stream = own["piece"][...].astype(F32)
             hat, unused = norm_parts(stream)
             normed = (hat * table[2 * layer : 2 * layer + 1, :] + table[4 + 2 * layer : 5 + 2 * layer, :]).astype(BF16)
             at = pl.ds(pl.multiple_of(step * rows, rows), rows)
@@ -798,7 +825,6 @@
     def tiled(i):
         return lax.rem(jnp.minimum(i, feed - 1), tiles)
 
-    tail = feed - tiles
     ins["expand"].spec = pl.BlockSpec((width, tile), lambda i: (0, tiled(i)))
     ins["expand_shift"].spec = pl.BlockSpec((1, tile), lambda i: (0, tiled(i)))
     ins["shrink"].spec = pl.BlockSpec((tile, width), lambda i: (tiled(i), 0))
@@ -809,7 +835,7 @@
         "value": Item(shaped((rows, width)), pl.BlockSpec((rows, lanes), lambda i: (0, jnp.maximum(i - first_key - pairs, 0)))),
         "middle": Item(shaped((rows, width), F32)),
         "small": Item(shaped((8, width), F32)),
-        "wide": Item(shaped((1, hidden), F32), pl.BlockSpec((1, tile), lambda i: (0, jnp.clip(i - tail, 0, tiles - 1)))),
+        "wide": Item(shaped((1, hidden), F32)),
     }
     scratch = {
         "active": pltpu.VMEM((rows, hidden), BF16),
@@ -844,7 +870,7 @@
         mixed_back, stats, held = own["mixed_back"], own["stats"], own["qkv_held"]
         sums = own["sums"] if encoder else outs["sums"]
         cores = Cores(here, sums, own["cores"], wide)
-        line = Line(here, [mixed_back, stats], own["line"])
+        line = Line(here, [mixed_back, stats], own["line"], None, (False, False))
         load = pltpu.make_async_copy(ins["qkv"], held, own["qkv_sem"].at[0])
         gain, shift = table[2 * layer + 1 : 2 * layer + 2, :], table[5 + 2 * layer : 6 + 2 * layer, :]
         extra.events(here, step, steps, ins, outs, own)
@@ -874,7 +900,7 @@
         def backward(n, steep):
             hidden_low = (steep * mm(low[...], ins["shrink"][...], NT)).astype(BF16)
             own["hidden_low"][:, columns_at(n)] = hidden_low
-            outs["wide"][...] = columns(hidden_low.astype(F32))
+            outs["wide"][:, columns_at(n)] = columns(hidden_low.astype(F32))
             back[...] += mm(hidden_low, ins["expand"][...], NT)
 
         if encoder:
@@ -1058,7 +1084,7 @@
     rows, width = ins["query"].array.shape
     fine = width // slots // PARTS
     units = 3
-    steps = 1 + units
+    steps = 2 + units
     ins["stream"].spec = pl.BlockSpec((1, rows, width), lambda i: (0, 0, 0))
     outs = {"small": Item(shaped((8, width), F32)), "sums": Item(shaped((4, PARTS, units, fine, width)))}
     if coded:
@@ -1081,7 +1107,17 @@
             def _():
                 cores.put(jnp.int32(n), mm(ins["normed"][...], sources[n][...], TN))
 
+        for n in range(units):
+
+            @at_step(step, n + 1)
+            def _():
+                cores.collect(jnp.int32(n))
+
         @at_step(step, units)
+        def _():
+            cores.finish(units)
+
+        @at_step(step, units + 1)
         def _():
             query, key, value = sources
             weight = ins["weight"]
@@ -1100,9 +1136,6 @@
                 outs["grad"][...] = start
             small += [jnp.zeros_like(small[0])] * (8 - len(small))
             outs["small"][...] = jnp.concatenate(small)
-            for n in range(units):
-                cores.collect(jnp.int32(n))
-            cores.finish(units)
 
         extra.closing(here, step, steps, ins, outs, own)
 
@@ -1110,20 +1143,32 @@
 
 
 def last_kernel(here, step, ins, outs, own):
-    square = Square(here, own["square"][0], own["square"][1:], ins["sums"])
-    stack = Stack(here, own["total"], own["stack"])
+    stacks = [Stack(here, ins[f"total{n}"], own[f"stack{n}"]) for n in range(3)]
     rows = Sum(here, [ins["small"]], own["sum"])
-    square.load()
     rows.begin()
-    square.start()
-    rows.meet(0)
-    rows.meet(1)
-    square.sides()
-    rows.meet(2)
+    for stack in stacks:
+        stack.start()
+    for stage in range(3):
+        rows.meet(stage)
+    for n, stack in enumerate(stacks):
+        stack.finish(outs["units"].at[pl.ds(n, 1)])
     rows.finish(outs["rows"])
-    square.total(own["total"])
-    stack.start()
-    stack.finish(outs["units"])
+
+
+def assemble_kernel(project0, project1, five, six, two, three, four, project, output, expand, shrink):
+    encoder = [(five, n) for n in range(five.shape[0])] + [(six, n) for n in range(six.shape[0])]
+    decoder = [(part, n) for part in (two, three, four) for n in range(part.shape[0])]
+    fine, width = project0.shape[1:]
+    for layer, units, triple in ((0, encoder, project0), (1, decoder, project1)):
+        for n in range(3):
+            project[layer, :, n * width : (n + 1) * width] = triple[n]
+        for n in range(4):
+            ref, at = units[n]
+            shrink[layer, n * fine : (n + 1) * fine, :] = ref[at]
+            ref, at = units[4 + n]
+            expand[layer, :, n * width : (n + 1) * width] = ref[at]
+        ref, at = units[8]
+        output[layer] = ref[at]
 
 
 class Nothing:
@@ -1139,23 +1184,28 @@
 
 class Beside(Nothing):
     def __init__(
-        self, slots, gathers=None, gather_steps=(), squares=None, stacks=None, sums=None, lines=None, line_steps=(), spreads=None, spread_steps=()
+        self, slots, gathers=None, gather_steps=(), squares=None, stacks=None, sums=None, lines=None, line_steps=(), spreads=None, spread_steps=(), hop=None
     ):
+        self.hop = hop
         self.lines, self.line_steps, self.spreads, self.spread_steps = lines or {}, line_steps, spreads or {}, spread_steps
         self.slots, self.gathers, self.gather_steps = slots, gathers or {}, gather_steps
         self.squares, self.stacks, self.sums = squares or {}, stacks or {}, sums or {}
 
     def declare(self, ins, outs, scratch):
+        if self.hop:
+            array = self.hop[1]
+            ins["hop"] = anywhere(array)
+            outs["hopped"] = anywhere(shaped(array.shape))
+            scratch["hop"] = Hop.scratch()
         for name, (array, layer) in self.gathers.items():
             block = (1,) + array.shape[1:]
             ins["shard_" + name] = Item(array, pl.BlockSpec(block, lambda i, layer=layer: (layer, 0, 0)))
             outs["gathered_" + name] = anywhere(shaped((self.slots, PARTS) + array.shape[1:]))
         if self.gathers:
             scratch["gather"] = Gather.scratch(len(self.gathers))
-        for name, (array, layer) in self.lines.items():
-            block = (1,) + array.shape[1:]
-            ins["line_" + name] = Item(array, pl.BlockSpec(block, lambda i, layer=layer: (layer, 0, 0)))
-            outs["lined_" + name] = anywhere(shaped((PARTS,) + array.shape[1:]))
+        for name, (item, absolute) in self.lines.items():
+            ins["line_" + name] = item
+            outs["lined_" + name] = anywhere(shaped((PARTS,) + item.spec.block_shape[1:]))
         if self.lines:
             scratch["lines"] = Line.scratch(len(self.lines)) + [DMA((len(self.lines),))]
         for name, array in self.spreads.items():
@@ -1183,13 +1233,20 @@
             scratch["stack_" + name] = Stack.scratch(shape[1], shape[2:])
         for name, (arrays, steps) in self.sums.items():
             for i, array in enumerate(arrays):
-                ins[f"sum_{name}{i}"] = Item(array)
+                if isinstance(array, str):
+                    arrays = arrays[:i] + [outs[array].array] + arrays[i + 1 :]
+                else:
+                    ins[f"sum_{name}{i}"] = Item(array)
             width = min(a.shape[1] for a in arrays)
             rows = -(-sum(a.shape[0] * (a.shape[1] // width) for a in arrays) // 16) * 16
             outs["summed_" + name] = Item(shaped((rows, width), F32))
             scratch["sum_" + name] = Sum.scratch(rows, width)
 
     def listed(self, here, ins, outs, own):
+        if self.hop:
+            hop_task = Hop(here, self.hop[0], ins["hop"], outs["hopped"], own["hop"])
+            yield self.hop[2], hop_task.start
+            yield None, hop_task.finish
         if self.gathers:
             names = list(self.gathers)
             gather = Gather(here, [ins["shard_" + n].at[0] for n in names], [outs["gathered_" + n] for n in names], own["gather"])
@@ -1215,8 +1272,10 @@
             sources = [ins["line_" + n].at[0] for n in line_names]
             arrays = [outs["lined_" + n] for n in line_names]
             sems = own["lines"]
-            line = Line(here, arrays, sems[:3], sources)
-            keeps = [pltpu.make_async_copy(sources[m], arrays[m].at[here.z], sems[3].at[m]) for m in range(len(line_names))]
+            line = Line(here, arrays, sems[:3], sources, [absolute for item, absolute in self.lines.values()])
+            keeps = [
+                pltpu.make_async_copy(sources[m], line.at(m, here.z, here.z), sems[3].at[m]) for m in range(len(line_names))
+            ]
 
             def begin():
                 for m in range(len(line_names)):
@@ -1264,7 +1323,8 @@
             yield steps[0], stack.start
             yield steps[1], functools.partial(stack.finish, outs["stacked_" + name])
         for name, (arrays, steps) in self.sums.items():
-            rows = Sum(here, [ins[f"sum_{name}{i}"] for i in range(len(arrays))], own["sum_" + name])
+            sources = [outs[a] if isinstance(a, str) else ins[f"sum_{name}{i}"] for i, a in enumerate(arrays)]
+            rows = Sum(here, sources, own["sum_" + name])
             yield steps[0], rows.begin
             for stage in range(3):
                 yield steps[1 + stage], functools.partial(rows.meet, stage)
@@ -1291,6 +1351,11 @@
         actions = self.grouped(here, ins, outs, own).get(None)
         if actions:
             self.play(step, steps - 1, actions)
+
+
+FORWARD1_GATHER = (0, 3, 6, 9, None, None)
+MIDDLE1_GATHER = (0, 5, 15, 21, 27, 31)
+FORWARD0_SQUARE = (0, 1, 4, None)
 
 
 def on_device(
@@ -1350,23 +1415,27 @@
         "decode": Item(decode_weight),
     }
     weights = {"project": project_weight, "output": output_weight, "expand": expand_weight, "shrink": shrink_weight}
-    ins["signs"], ins["patches"] = Item(signs), Item(patches)
-    for name, array in weights.items():
-        ins[name] = Item(array, pl.BlockSpec((1,) + array.shape[1:], lambda i: (1, 0, 0)))
+
+    def shard(name, layer):
+        array = weights[name]
+        return Item(array, pl.BlockSpec((1,) + array.shape[1:], lambda i: (layer, 0, 0)))
+
+    ins["signs"], ins["patches"], ins["project"] = Item(signs), Item(patches), shard("project", 1)
     outs = {
         "table": anywhere(shaped((slots, parts, 64, fine), F32)),
+        "project": anywhere(shaped((slots, parts) + project_weight.shape[1:])),
         "signs": anywhere(shaped((parts, rows, CODE))),
         "patches": anywhere(shaped((parts, rows, width))),
     }
-    for name, array in weights.items():
-        outs[name] = anywhere(shaped((slots, parts) + array.shape[1:]))
+    names = ("output", "expand", "shrink")
     scratch = {
         "table": pltpu.VMEM((64, fine), F32),
-        "gather": Gather.scratch(5),
-        "line": Line.scratch(2),
-        "keep": DMA((2,)),
+        "gather": Gather.scratch(2),
+        "line": Line.scratch(1),
+        "keep": DMA((1,)),
+        "patches": Hop.scratch(),
     }
-    first = run(first_kernel, 1, ins, outs, scratch, 0, "first_gather", 70)
+    first = run(first_kernel, 1, ins, outs, scratch, 0, "first_gather", 30)
 
     small = first["table"].reshape(devices, 64, fine)
     table = small.transpose(1, 0, 2).reshape(64, width)
@@ -1379,9 +1448,12 @@
     def flat(array):
         return array.reshape(-1, array.shape[-1])
 
+    def piece(array, n):
+        return Item(array, pl.BlockSpec((1, rows, width), lambda i: (n, 0, 0)))
+
     def forward(layer, pieces, weight, extra, collective):
         ins = {
-            "pieces": Item(pieces),
+            **pieces,
             "table": Item(table),
             "weight": Item(weight),
             "segment_row": Item(segment_row),
@@ -1420,40 +1492,32 @@
         ins.update({k: Item(v) for k, v in more.items()})
         return projection_back(layer == 1, layer, slots, ins, extra, collective)
 
-    decoder = {n: flat(first[n]) for n in weights}
-    names = ("output", "expand", "shrink")
+    decoder = {"project": flat(first["project"])}
+    beside = Beside(slots, {n: (weights[n], 1) for n in names}, FORWARD1_GATHER, hop=(2, first["patches"], 1))
+    ahead1 = forward(1, {"pieces": Item(first["signs"])}, decoder["project"], beside, 1)
+    decoder.update({n: flat(ahead1["gathered_" + n]) for n in names})
+
+    beside = Beside(slots, {n: (weights[n], 0) for n in weights}, MIDDLE1_GATHER)
+    stream1 = ahead1["stream"][None]
+    between1 = middle(1, stream1, cotangent[0], ahead1, decoder, beside, 2)
+    encoder = {n: flat(between1["gathered_" + n]) for n in weights}
+    beside = Beside(slots, squares={"two": (between1["sums"], 0, 3, (0, 1, 3, None))}, hop=(3, ahead1["hopped"], 0))
+    after1 = projection(1, stream1, ahead1, between1, decoder["project"], beside, 3, pieces=first["signs"])
+
     beside = Beside(
         slots,
-        {"project": (project_weight, 0)},
-        (0, 2, 4, 5, 7, 9),
-        lines={n: (weights[n], 0) for n in names},
-        line_steps=(1, 4, 7, None),
-    )
-    ahead1 = forward(1, first["signs"], decoder["project"], beside, 1)
-    encoder = {"project": flat(ahead1["gathered_project"])}
-
-    beside = Beside(
-        slots,
-        spreads={n: ahead1["lined_" + n] for n in names},
-        spread_steps=(0, 12, 18, None),
-        squares={"two": (None, 0, 4, (None, 13, 20, 27))},
-    )
-    stream1 = ahead1["stream"][None]
-    between1 = middle(1, stream1, cotangent[0], ahead1, decoder, beside, 2)
-    encoder.update({n: flat(between1["gathered_" + n]) for n in names})
-    beside = Beside(slots, stacks={"two": (between1["total_two"], (0, 3))})
-    after1 = projection(1, stream1, ahead1, between1, decoder["project"], beside, 3, pieces=first["signs"])
-
-    beside = Beside(
-        slots,
-        squares={"three": (between1["sums"], 4, 5, (0, 1, 5, None))},
-        sums={"one": ([after1["small"], between1["small"], between1["wide"], after1["decode_grad"]], (0, 1, 3, 5, None))},
-    )
-    ahead0 = forward(0, first["patches"], encoder["project"], beside, 4)
+        squares={"three": (between1["sums"], 3, 5, FORWARD0_SQUARE)},
+        stacks={"two": (after1["total_two"], (0, 6))},
+        sums={"one": ([after1["small"], between1["small"], between1["wide"], after1["decode_grad"]], (0, 1, 3, 6, None))},
+    )
+    pieces = [piece(patches, 0), piece(first["patches"], 1), piece(ahead1["hopped"], 2)]
+    pieces += [piece(first["patches"], 3), piece(after1["hopped"], 3)]
+    ahead0 = forward(0, {f"piece{n}": item for n, item in enumerate(pieces)}, encoder["project"], beside, 4)
     beside = Beside(
         slots,
         squares={
             "one": (after1["sums"], 0, 3, (0, 1, 4, 9)),
+            "four": (between1["sums"], 8, 1, (0, 1, 4, 9)),
             "five": (None, 0, 4, (None, 18, 22, 28)),
             "six": (None, 4, 5, (None, 22, 30, None)),
         },
@@ -1462,27 +1526,34 @@
             "one": ("one", (10, 18)),
             "five": ("five", (33, None)),
         },
-    )
-    between0 = middle(0, first["patches"], after1["unit_grad"], ahead0, encoder, beside, 5)
+        sums={"two": (["small", "wide", "code_grad"], (13, 15, 17, 20, 28))},
+    )
+    between0 = middle(0, patches, after1["unit_grad"], ahead0, encoder, beside, 5)
     beside = Beside(
         slots,
-        stacks={"six": (between0["total_six"], (0, 3))},
-        sums={"two": ([between0["small"], between0["wide"], between0["code_grad"]], (0, 1, 2, 3, None))},
-    )
-    after0 = projection(0, first["patches"], ahead0, between0, encoder["project"], beside, 6)
-
-    ins = {"sums": anywhere(after0["sums"]), "small": Item(after0["small"])}
+        squares={f"seven{n}": (None, n, 1, (None, n + 2, 4, None)) for n in range(3)},
+        stacks={n: (between0["total_" + n], (0, None)) for n in ("six", "four")},
+    )
+    after0 = projection(0, patches, ahead0, between0, encoder["project"], beside, 6)
+
+    ins = {f"total{n}": Item(after0[f"total_seven{n}"]) for n in range(3)}
+    ins["small"] = Item(after0["small"])
     outs = {"units": Item(shaped((3, fine, width), F32)), "rows": Item(shaped((16, width), F32))}
-    scratch = {
-        "square": Square.scratch(3, (fine, width), True),
-        "total": pltpu.VMEM((parts, 3, fine, width), BF16),
-        "stack": Stack.scratch(3, (fine, width)),
-        "sum": Sum.scratch(16, width),
-    }
-    last = run(last_kernel, 1, ins, outs, scratch, 7, "last_sums", 30)
+    scratch = {f"stack{n}": Stack.scratch(1, (fine, width)) for n in range(3)}
+    scratch["sum"] = Sum.scratch(16, width)
+    last = run(last_kernel, 1, ins, outs, scratch, 7, "last_sums", 20)
+
+    units = [last["units"], between0["stacked_one"], between0["stacked_five"], after0["stacked_six"]]
+    units += [ahead0["stacked_two"], between0["stacked_three"], after0["stacked_four"]]
+    project_grad, output_grad, expand_grad, shrink_grad = pl.pallas_call(
+        assemble_kernel,
+        out_shape=tuple(shaped(weights[n].shape, F32) for n in ("project", "output", "expand", "shrink")),
+        compiler_params=pltpu.CompilerParams(vmem_limit_bytes=BIG),
+        name="assemble",
+    )(*units)
 
     device = slot * parts + z
-    one, two = ahead0["summed_one"], after0["summed_two"]
+    one, two = ahead0["summed_one"], between0["summed_two"]
     summed = jnp.concatenate([last["rows"][:8], one, two])
     mine = lax.dynamic_slice(summed, (0, device * fine), (summed.shape[0], fine))
     in0, in1, mid1 = mine[0:4], mine[8:13], mine[16:20]
@@ -1490,28 +1561,18 @@
     mid0, decode_grad, code_grad = mine[at : at + 4], mine[28:46], mine[at + 12 : at + 30]
     wide = jnp.stack([two[8:12].reshape(hidden), one[16:20].reshape(hidden)])
     wide = lax.dynamic_slice(wide, (0, device * (hidden // devices)), (2, hidden // devices))
-    decoder_mlp = jnp.concatenate([after1["stacked_two"], between0["stacked_three"]])
-    encoder_mlp = jnp.concatenate([between0["stacked_five"], after0["stacked_six"]])
-    encoder_project, decoder_project = last["units"], between0["stacked_one"]
-
-    def both(cut):
-        return jnp.stack([cut(encoder_mlp), cut(decoder_mlp)])
-
-    def joined(units):
-        return units.transpose(1, 0, 2).reshape(fine, units.shape[0] * width)
-
     return (
         between1["decoded"][None],
         after0["grad"][None],
         jnp.stack([jnp.stack([in0[0], mid0[0]]), jnp.stack([in1[0], mid1[0]])]),
         jnp.stack([jnp.stack([in0[1], mid0[1]]), jnp.stack([in1[1], mid1[1]])]),
-        jnp.stack([joined(encoder_project), joined(decoder_project)]),
+        project_grad,
         jnp.stack([in0[2:4], in1[2:4]]),
-        both(lambda g: g[8]),
+        output_grad,
         jnp.stack([mid0[2], mid1[2]]),
-        both(lambda g: joined(g[4:8])),
+        expand_grad,
         wide,
-        both(lambda g: g[0:4].reshape(4 * fine, width)),
+        shrink_grad,
         jnp.stack([mid0[3], mid1[3]]),
         code_grad.T,
         decode_grad,

time: 483 us -> 450 us (0.932)
  Pallas kernels: 450 us -> 425 us
    pallas_call x8, Pallas kernels: 450 us -> 423 us  [run(): pl.pallas_call(kernel, grid=(steps,), in_specs=[i.spec for i in ins.value...]
where the time goes in v3:
time: 450 us; the launch traced here: 443 us
  Pallas kernels  425 us (94%)
  local copies, waits for them, and re-layouts  12.4 us (3%)
  other arithmetic  4.55 us (1%)
    pallas_call x8, Pallas kernels, run(): pl.pallas_call(kernel, grid=(steps,), in_specs=[i.spec for i in ins.value...  423 us

profile of v3, /device:TPU:0, one launch (start us, length us, event | category | flops | bytes accessed | tf_op | source)
XLA Modules:
  0.0 443.5 jit_solution(15205339799091259162)
XLA Ops:
  0.7 0.7 reduce
  1.4 0.6 gather_fusion
  2.0 0.6 copy.75
  2.6 0.8 fusion.5
  3.3 0.8 copy.58.refs_9_
  4.1 0.8 copy.61.refs_4_.refs_11_.refs_8_
  4.9 47.0 %first_gather.1 = (f32[8,4,64,24]{3,2,1,0:T(8,128)}, bf16[8,4,24,2304]{3,2,1,0:T(8,128)(2,1)}, bf16[4,384,18]{2,1,0:T(8,128)(2,1)}, bf16[4,384,768]{2,1,0:T(8,128)(2,1)}) custom-call(bf16[2,2,24]{2,1,0:T(2,128)(2,1)} %refs_0_.3, bf16[2,2,24]{2,1,0:T(2,128)(2,1)} %refs_1_.1, bf16[2,2,24]{2,1,0:T(2,128)(2,1)} %refs_2_.1, bf16[2,24]{1,0:T(2,128)(2,1)} %refs_3_.1, ...), custom_call_target="tpu_custom_call" | custom-call | flops 34500001792 | tf_op jit(solution)/shard_map/first_gather/pallas_call | solution.py:647
  51.9 1.0 slice.120
  52.9 1.5 copy.59
  54.4 0.1 copy.74
  54.5 0.8 copy.60.refs_1_.refs_5_.refs_6_
  55.5 0.7 squeeze.14.refs_8_
  56.3 0.7 squeeze.13.refs_8_
  57.0 64.1 %forward_attention.2 = (bf16[1536,2304]{1,0:T(8,128)(2,1)}, bf16[384,768]{1,0:T(8,128)(2,1)}, bf16[384,768]{1,0:T(8,128)(2,1)}, f32[384,128]{1,0:T(8,128)}, f32[...) custom-call(bf16[4,384,18]{2,1,0:T(8,128)(2,1)} %get-tuple-element.7, ...), custom_call_target="tpu_custom_call" | custom-call | flops 34500001792 | tf_op jit(solution)/shard_map/forward_attention/pallas_call | solution.py:647
  121.1 94.8 %decoder_middle.1 = (bf16[384,768]{1,0:T(8,128)(2,1)}, bf16[384,768]{1,0:T(8,128)(2,1)}, bf16[384,768]{1,0:T(8,128)(2,1)}, f32[384,768]{1,0:T(8,128)}, f32[8,768...) custom-call(f32[1,384,768]{2,1,0:T(8,128)} %bitcast.75, ...), custom_call_target="tpu_custom_call" | custom-call | flops 92000002048 | tf_op jit(solution)/shard_map/decoder_middle/pallas_call | solution.py:647
  215.9 25.2 %projection_back.2 = (f32[8,768]{1,0:T(8,128)}, bf16[4,4,3,24,768]{4,3,2,1,0:T(8,128)(2,1)}, f32[384,18]{1,0:T(8,128)}, f32[18,768]{1,0:T(8,128)}, bf16[4,384,76...) custom-call(bf16[384,768]{1,0:T(8,128)(2,1)} %get-tuple-element.89.refs_0_, bf16[384,768]{1,0:T(8,128)(2,1)} %get-tuple-element.90.refs_1_, ...), custom_call_target="tpu_custom_call" | custom-call | flops 13799999488 | tf_op jit(solution)/shard_map/projection_back/pallas_call | solution.py:647
  241.1 41.7 %forward_attention.3 = (bf16[1536,2304]{1,0:T(8,128)(2,1)}, bf16[384,768]{1,0:T(8,128)(2,1)}, bf16[384,768]{1,0:T(8,128)(2,1)}, f32[384,128]{1,0:T(8,128)}, bf16...) custom-call(bf16[1,384,768]{2,1,0:T(8,128)(2,1)} %refs_4_.3, ...), custom_call_target="tpu_custom_call" | custom-call | flops 34500001792 | tf_op jit(solution)/shard_map/forward_attention/pallas_call | solution.py:647
  282.9 102.2 %encoder_middle.1 = (bf16[384,768]{1,0:T(8,128)(2,1)}, bf16[384,768]{1,0:T(8,128)(2,1)}, bf16[384,768]{1,0:T(8,128)(2,1)}, f32[384,768]{1,0:T(8,128)}, f32[8,768...) custom-call(bf16[1,384,768]{2,1,0:T(8,128)(2,1)} %refs_4_.3, ...), custom_call_target="tpu_custom_call" | custom-call | flops 92000002048 | tf_op jit(solution)/shard_map/encoder_middle/pallas_call | solution.py:647
  385.1 30.8 %projection_back.3 = (f32[8,768]{1,0:T(8,128)}, bf16[4,4,3,24,768]{4,3,2,1,0:T(8,128)(2,1)}, f32[384,768]{1,0:T(8,128)}, bf16[4,1,24,768]{3,2,1,0:T(8,128)(2,1)}...) custom-call(bf16[384,768]{1,0:T(8,128)(2,1)} %get-tuple-element.111., ...), custom_call_target="tpu_custom_call" | custom-call | flops 13799999488 | tf_op jit(solution)/shard_map/projection_back/pallas_call | solution.py:647
  416.0 0.6 fusion.6
  416.6 17.0 %last_sums.1 = (f32[3,24,768]{2,1,0:T(8,128)}, f32[16,768]{1,0:T(8,128)}) custom-call(bf16[4,1,24,768]{3,2,1,0:T(8,128)(2,1)} %get-tuple-element.119.refs_0_, bf16[4,1,24,768]{3,2,1,0:T(8,128)(2,1)} %get-tuple-element.120.refs_1_, bf16[4,1,24,768]{3,2,1,0:T(8,128)(2,1)} %get-tuple-element.121.refs_2_, f32[8,768]{1,0:T(8,128)} %get-tuple-element.122.refs_3_), custom_call_target="tpu_custom_call" | custom-call | flops 23000000512 | tf_op jit(solution)/shard_map/last_sums/pallas_call | solution.py:647
  433.6 0.9 slice.97
  434.6 0.6 pad_maximum_fusion.2
  435.2 0.5 slice_bitcast_fusion.6
  435.7 0.6 fusion.9
  436.3 0.6 pad_maximum_fusion.3
  436.9 0.6 pad_maximum_fusion.1
  437.5 0.6 pad_maximum_fusion
  438.1 0.7 copy.73
  438.7 2.7 assemble.1
  441.4 0.8 copy.89
  442.2 1.0 copy.90
  (23 shorter events, 0.4 us)
Async XLA Ops:
  385.1 30.8 %copy-start.3 = (f32[32,768]{1,0:T(8,128)S(1)}, f32[32,768]{1,0:T(8,128)}, u32[]{:S(2)}) copy-start(f32[32,768]{1,0:T(8,128)} %get-tuple-element.125) | copy-start | bytes 294916
  385.1 30.8 %copy-start.2 = (f32[48,768]{1,0:T(8,128)S(1)}, f32[48,768]{1,0:T(8,128)}, u32[]{:S(2)}) copy-start(f32[48,768]{1,0:T(8,128)} %get-tuple-element.124) | copy-start | bytes 442372
  433.6 7.8 %copy-start.1 = (bf16[384,768]{1,0:T(8,128)(2,1)S(1)}, bf16[384,768]{1,0:T(8,128)(2,1)}, u32[]{:S(2)}) copy-start(bf16[384,768]{1,0:T(8,128)(2,1)} %get-tuple-element.87) | copy-start | bytes 1769476
  433.6 8.6 %copy-start = (f32[384,768]{1,0:T(8,128)S(1)}, f32[384,768]{1,0:T(8,128)}, u32[]{:S(2)}) copy-start(f32[384,768]{1,0:T(8,128)} %get-tuple-element.118) | copy-start | bytes 3538948

commit v4 on v3

--- a/solution.py
+++ b/solution.py
@@ -683,28 +683,33 @@
         table[17 + i : 18 + i, :] = wide[i // 4 : i // 4 + 1, fine * (i % 4) : fine * (i % 4 + 1)]
     table[25:43, :] = ins["encode"][...].astype(F32).T
     table[43:61, :] = ins["decode"][...].astype(F32)
-    gather = Gather(here, [table, ins["project"].at[0]], [outs["table"], outs["project"]], own["gather"])
+    gather = Gather(
+        here,
+        [table, ins["project"].at[0], ins["output"].at[0]],
+        [outs["table"], outs["project"], outs["output"]],
+        own["gather"],
+    )
     signs = ins["signs"].at[0]
     line = Line(here, [outs["signs"]], own["line"], [signs], (False,))
     keep = pltpu.make_async_copy(signs, outs["signs"].at[0], own["keep"].at[0])
     patches = Hop(here, 1, ins["patches"].at[0], outs["patches"], own["patches"])
-    for m in range(2):
+    for m in range(3):
         gather.start(m)
     line.start(0)
     keep.start()
     patches.start()
     for k in range(1, PARTS):
-        for m in range(2):
+        for m in range(3):
             gather.hop(m, k)
         line.hop(0, k)
-        for m in range(2):
+        for m in range(3):
             gather.turn(m, k - 1)
-    for m in range(2):
+    for m in range(3):
         gather.turn(m, PARTS - 1)
         gather.siblings(m)
-    for m in range(2):
+    for m in range(3):
         gather.corner(m)
-    for m in range(2):
+    for m in range(3):
         gather.finish(m)
     line.finish(0)
     patches.finish()
@@ -986,7 +991,7 @@
             cores.collect(unit - 1)
             cores.finish(units)
 
-        for n, k in ((units - 1, 1), (units + 3, 2)):
+        for n, k in ((units, 1), (units + 5, 2)):
 
             @pl.when(unit == n)
             def _():
@@ -1420,17 +1425,19 @@
         array = weights[name]
         return Item(array, pl.BlockSpec((1,) + array.shape[1:], lambda i: (layer, 0, 0)))
 
-    ins["signs"], ins["patches"], ins["project"] = Item(signs), Item(patches), shard("project", 1)
+    ins["signs"], ins["patches"] = Item(signs), Item(patches)
+    ins["project"], ins["output"] = shard("project", 1), shard("output", 1)
     outs = {
         "table": anywhere(shaped((slots, parts, 64, fine), F32)),
         "project": anywhere(shaped((slots, parts) + project_weight.shape[1:])),
+        "output": anywhere(shaped((slots, parts) + output_weight.shape[1:])),
         "signs": anywhere(shaped((parts, rows, CODE))),
         "patches": anywhere(shaped((parts, rows, width))),
     }
-    names = ("output", "expand", "shrink")
+    names = ("expand", "shrink")
     scratch = {
         "table": pltpu.VMEM((64, fine), F32),
-        "gather": Gather.scratch(2),
+        "gather": Gather.scratch(3),
         "line": Line.scratch(1),
         "keep": DMA((1,)),
         "patches": Hop.scratch(),
@@ -1492,7 +1499,7 @@
         ins.update({k: Item(v) for k, v in more.items()})
         return projection_back(layer == 1, layer, slots, ins, extra, collective)
 
-    decoder = {"project": flat(first["project"])}
+    decoder = {n: flat(first[n]) for n in ("project", "output")}
     beside = Beside(slots, {n: (weights[n], 1) for n in names}, FORWARD1_GATHER, hop=(2, first["patches"], 1))
     ahead1 = forward(1, {"pieces": Item(first["signs"])}, decoder["project"], beside, 1)
     decoder.update({n: flat(ahead1["gathered_" + n]) for n in names})

time: 450 us -> 447 us (level)
  no operation moved by 1% of the time
where the time goes in v4:
time: 447 us; the launch traced here: 440 us
  Pallas kernels  422 us (94%)
  local copies, waits for them, and re-layouts  12.4 us (3%)
  other arithmetic  4.55 us (1%)
    pallas_call x8, Pallas kernels, run(): pl.pallas_call(kernel, grid=(steps,), in_specs=[i.spec for i in ins.value...  419 us

profile of v4, /device:TPU:0, one launch (start us, length us, event | category | flops | bytes accessed | tf_op | source)
XLA Modules:
  0.0 440.1 jit_solution(3485843227921584651)
XLA Ops:
  0.7 0.7 reduce
  1.4 0.6 gather_fusion
  2.0 0.6 copy.75
  2.6 0.8 fusion.5
  3.3 0.8 copy.58.refs_9_
  4.1 0.8 copy.61.refs_4_.refs_11_.refs_8_
  4.9 49.5 %first_gather.1 = (f32[8,4,64,24]{3,2,1,0:T(8,128)}, bf16[8,4,24,2304]{3,2,1,0:T(8,128)(2,1)}, bf16[8,4,24,768]{3,2,1,0:T(8,128)(2,1)}, bf16[4,384,18]{2,1,0:T(8,128)(2,1)}, bf16[4,384,768]{2,1,0:T(8,128)(2,1)}) custom-call(bf16[2,2,24]{2,1,0:T(2,128)(2,1)} %refs_0_.3, bf16[2,2,24]{2,1,0:T(2,128)(2,1)} %refs_1_.1, bf16[2,2,24]{2,1,0:T(2,128)(2,1)} %refs_2_.1, ...), custom_call_target="tpu_custom_call" | custom-call | flops 34500001792 | tf_op jit(solution)/shard_map/first_gather/pallas_call | solution.py:647
  54.4 1.0 slice.120
  55.4 1.5 copy.59
  56.9 0.1 copy.74
  57.0 0.8 copy.60.refs_1_.refs_5_.refs_6_
  58.0 0.7 squeeze.14.refs_8_
  58.8 0.7 squeeze.13.refs_8_
  59.5 60.6 %forward_attention.2 = (bf16[1536,2304]{1,0:T(8,128)(2,1)}, bf16[384,768]{1,0:T(8,128)(2,1)}, bf16[384,768]{1,0:T(8,128)(2,1)}, f32[384,128]{1,0:T(8,128)}, f32[...) custom-call(bf16[4,384,18]{2,1,0:T(8,128)(2,1)} %get-tuple-element.7, ...), custom_call_target="tpu_custom_call" | custom-call | flops 34500001792 | tf_op jit(solution)/shard_map/forward_attention/pallas_call | solution.py:647
  120.1 98.8 %decoder_middle.1 = (bf16[384,768]{1,0:T(8,128)(2,1)}, bf16[384,768]{1,0:T(8,128)(2,1)}, bf16[384,768]{1,0:T(8,128)(2,1)}, f32[384,768]{1,0:T(8,128)}, f32[8,768...) custom-call(f32[1,384,768]{2,1,0:T(8,128)} %bitcast.76, ...), custom_call_target="tpu_custom_call" | custom-call | flops 92000002048 | tf_op jit(solution)/shard_map/decoder_middle/pallas_call | solution.py:647
  218.9 24.0 %projection_back.2 = (f32[8,768]{1,0:T(8,128)}, bf16[4,4,3,24,768]{4,3,2,1,0:T(8,128)(2,1)}, f32[384,18]{1,0:T(8,128)}, f32[18,768]{1,0:T(8,128)}, bf16[4,384,76...) custom-call(bf16[384,768]{1,0:T(8,128)(2,1)} %get-tuple-element.89.refs_0_, bf16[384,768]{1,0:T(8,128)(2,1)} %get-tuple-element.90.refs_1_, ...), custom_call_target="tpu_custom_call" | custom-call | flops 13799999488 | tf_op jit(solution)/shard_map/projection_back/pallas_call | solution.py:647
  242.9 41.1 %forward_attention.3 = (bf16[1536,2304]{1,0:T(8,128)(2,1)}, bf16[384,768]{1,0:T(8,128)(2,1)}, bf16[384,768]{1,0:T(8,128)(2,1)}, f32[384,128]{1,0:T(8,128)}, bf16...) custom-call(bf16[1,384,768]{2,1,0:T(8,128)(2,1)} %refs_4_.3, ...), custom_call_target="tpu_custom_call" | custom-call | flops 34500001792 | tf_op jit(solution)/shard_map/forward_attention/pallas_call | solution.py:647
  284.0 97.4 %encoder_middle.1 = (bf16[384,768]{1,0:T(8,128)(2,1)}, bf16[384,768]{1,0:T(8,128)(2,1)}, bf16[384,768]{1,0:T(8,128)(2,1)}, f32[384,768]{1,0:T(8,128)}, f32[8,768...) custom-call(bf16[1,384,768]{2,1,0:T(8,128)(2,1)} %refs_4_.3, ...), custom_call_target="tpu_custom_call" | custom-call | flops 92000002048 | tf_op jit(solution)/shard_map/encoder_middle/pallas_call | solution.py:647
  381.5 31.6 %projection_back.3 = (f32[8,768]{1,0:T(8,128)}, bf16[4,4,3,24,768]{4,3,2,1,0:T(8,128)(2,1)}, f32[384,768]{1,0:T(8,128)}, bf16[4,1,24,768]{3,2,1,0:T(8,128)(2,1)}...) custom-call(bf16[384,768]{1,0:T(8,128)(2,1)} %get-tuple-element.111., ...), custom_call_target="tpu_custom_call" | custom-call | flops 13799999488 | tf_op jit(solution)/shard_map/projection_back/pallas_call | solution.py:647
  413.2 0.6 fusion.6
  413.8 16.4 %last_sums.1 = (f32[3,24,768]{2,1,0:T(8,128)}, f32[16,768]{1,0:T(8,128)}) custom-call(bf16[4,1,24,768]{3,2,1,0:T(8,128)(2,1)} %get-tuple-element.119.refs_0_, bf16[4,1,24,768]{3,2,1,0:T(8,128)(2,1)} %get-tuple-element.120.refs_1_, bf16[4,1,24,768]{3,2,1,0:T(8,128)(2,1)} %get-tuple-element.121.refs_2_, f32[8,768]{1,0:T(8,128)} %get-tuple-element.122.refs_3_), custom_call_target="tpu_custom_call" | custom-call | flops 23000000512 | tf_op jit(solution)/shard_map/last_sums/pallas_call | solution.py:647
  430.2 0.9 slice.97
  431.2 0.6 pad_maximum_fusion.2
  431.8 0.5 slice_bitcast_fusion.6
  432.3 0.6 fusion.9
  432.9 0.6 pad_maximum_fusion.3
  433.5 0.6 pad_maximum_fusion.1
  434.1 0.6 pad_maximum_fusion
  434.7 0.7 copy.73
  435.3 2.7 assemble.1
  438.0 0.8 copy.89
  438.8 1.0 copy.90
  (23 shorter events, 0.4 us)
Async XLA Ops:
  381.4 31.6 %copy-start.3 = (f32[32,768]{1,0:T(8,128)S(1)}, f32[32,768]{1,0:T(8,128)}, u32[]{:S(2)}) copy-start(f32[32,768]{1,0:T(8,128)} %get-tuple-element.125) | copy-start | bytes 294916
  381.5 31.7 %copy-start.2 = (f32[48,768]{1,0:T(8,128)S(1)}, f32[48,768]{1,0:T(8,128)}, u32[]{:S(2)}) copy-start(f32[48,768]{1,0:T(8,128)} %get-tuple-element.124) | copy-start | bytes 442372
  430.2 7.8 %copy-start.1 = (bf16[384,768]{1,0:T(8,128)(2,1)S(1)}, bf16[384,768]{1,0:T(8,128)(2,1)}, u32[]{:S(2)}) copy-start(bf16[384,768]{1,0:T(8,128)(2,1)} %get-tuple-element.87) | copy-start | bytes 1769476
  430.2 8.6 %copy-start = (f32[384,768]{1,0:T(8,128)S(1)}, f32[384,768]{1,0:T(8,128)}, u32[]{:S(2)}) copy-start(f32[384,768]{1,0:T(8,128)} %get-tuple-element.118) | copy-start | bytes 3538948
